TPU v7x, 32 devices: a whole 2x2x4 slice. The times are simulated.
32 devices in a mesh: tile: 4 (over z), orbit: 8 (over y, x, core).
Axes of the slice: x: 2, y: 2, z: 4, core: 2. Of those that a mesh axis runs over, the one named last changes fastest.
Arguments:
- jacobians: bfloat16 [4096, 128, 3, 128], P(('tile', 'orbit')), may hold values from -1.5 to 1.5
- point_normals: float32 [4096, 6, 128], P(('tile', 'orbit')), as said below
- block_counts: int32 [32, 128], P(('tile', 'orbit')), may hold values from 1 to 128, 8192 in all within a row
- pair_owner: int32 [4096, 1], P(('tile', 'orbit')), may hold values from 0 to 7; in each aligned block of 128 rows (0 to 127, 128 to 255, ...) at most 32 rows name the same one
- pair_local: int32 [4096], P(('tile', 'orbit')), may hold values from 0 to 255
- crossing: int32 [8], replicated, may hold values from 0 to 7, as said below
Outputs:
- coupled: float32 [8, 256, 4096], P('orbit', 'tile')
Inputs may be any that keep to these rules, and one draw needn't show every extreme that they name: `point_normals`: each 3x3 block is symmetric, and in every row the diagonal entry exceeds the sum of the off-diagonal magnitudes by 0.2 or more. `pair_owner`: among the 128 rows of one device no owner appears more than 32 times. crossing[crossing[o]] = o and crossing[o] != o for every orbit o.
All inputs are finite; a program needn't handle non-finite values.
Results may differ from a plain program's by a relative error of at most 0.0029.
Values sent between devices are 32-bit elements; how exact they have to be, the bound alone decides.
A program may use at most 128 MiB of HBM per device.

v0:
```python
import jax
import jax.numpy as jnp
from jax import lax
from jax.sharding import PartitionSpec as P

PAIR_ORB = 256


def eliminate(jacobians, point_normals, counts, params):
    points = jacobians.shape[1]
    left_half = jacobians[..., :params]
    right_half = jacobians[..., params:].astype(jnp.float32)
    diag_one = point_normals[:, 0, :][:, :, None]
    diag_two = point_normals[:, 1, :][:, :, None]
    diag_three = point_normals[:, 2, :][:, :, None]
    off_ab = point_normals[:, 3, :][:, :, None]
    off_ac = point_normals[:, 4, :][:, :, None]
    off_bc = point_normals[:, 5, :][:, :, None]
    cof_aa = diag_two * diag_three - off_bc * off_bc
    cof_bb = diag_one * diag_three - off_ac * off_ac
    cof_cc = diag_one * diag_two - off_ab * off_ab
    cof_ab = off_ac * off_bc - off_ab * diag_three
    cof_ac = off_ab * off_bc - off_ac * diag_two
    cof_bc = off_ab * off_ac - diag_one * off_bc
    determinant = diag_one * cof_aa + off_ab * cof_ab + off_ac * cof_ac
    live_mask = (jnp.arange(points, dtype=jnp.int32)[None, :] < counts[:, None]).astype(jnp.float32)
    weight = live_mask[:, :, None] / determinant
    comp_a = right_half[:, :, 0, :]
    comp_b = right_half[:, :, 1, :]
    comp_c = right_half[:, :, 2, :]
    solved = jnp.stack(
        [
            (cof_aa * comp_a + cof_ab * comp_b + cof_ac * comp_c) * weight,
            (cof_ab * comp_a + cof_bb * comp_b + cof_bc * comp_c) * weight,
            (cof_ac * comp_a + cof_bc * comp_b + cof_cc * comp_c) * weight,
        ],
        axis=2,
    ).astype(jnp.bfloat16)
    blocks = jnp.einsum("spci,spcj->sij", left_half, solved, preferred_element_type=jnp.float32)
    return blocks.reshape(blocks.shape[0], params * params)


def local(jacobians, point_normals, block_counts, pair_owner, pair_local, crossing):
    slot_count = jacobians.shape[0]
    params = jacobians.shape[3] // 2
    square = params * params
    blocks = eliminate(jacobians, point_normals, block_counts[0], params)
    orbits = lax.axis_size("orbit")
    capacity = 2 * slot_count // orbits
    owners = pair_owner[:, 0]
    onehot = (owners[:, None] == jnp.arange(orbits, dtype=jnp.int32)[None, :]).astype(jnp.int32)
    before = jnp.cumsum(onehot, axis=0) - onehot
    slot_rank = jnp.sum(before * onehot, axis=1)
    target = owners * capacity + slot_rank
    outgoing = jnp.zeros((orbits * capacity, square), jnp.float32).at[target].set(blocks)
    outgoing = outgoing.reshape(orbits, capacity, square)
    labels = (
        jnp.full((orbits * capacity,), PAIR_ORB, jnp.float32)
        .at[target]
        .set(pair_local.astype(jnp.float32))
    )
    labels = labels.reshape(orbits, capacity)
    flipped = jnp.swapaxes(outgoing[crossing].reshape(orbits, capacity, params, params), 2, 3)
    flipped = flipped.reshape(orbits, capacity, square)
    arrived, arrived_flip, tag_rows, tag_flip = (
        lax.all_to_all(outgoing, "orbit", split_axis=0, concat_axis=0, tiled=True),
        lax.all_to_all(flipped, "orbit", split_axis=0, concat_axis=0, tiled=True),
        lax.all_to_all(labels, "orbit", split_axis=0, concat_axis=0, tiled=True),
        lax.all_to_all(labels[crossing], "orbit", split_axis=0, concat_axis=0, tiled=True),
    )
    gathered = jnp.concatenate([arrived, arrived_flip], axis=0).reshape(-1, square)
    pair_tags = jnp.concatenate([tag_rows, tag_flip], axis=0).reshape(-1).astype(jnp.int32)
    dense_sums = jax.ops.segment_sum(gathered, pair_tags, num_segments=PAIR_ORB)
    owned_share = lax.psum_scatter(dense_sums, "tile", scatter_dimension=0, tiled=True)
    return owned_share[None]


def solution(mesh):
    in_specs = (
        P(("tile", "orbit"), None, None, None),
        P(("tile", "orbit"), None, None),
        P(("tile", "orbit"), None),
        P(("tile", "orbit"), None),
        P(("tile", "orbit")),
        P(),
    )
    out_specs = P("orbit", "tile", None)
    return jax.shard_map(local, mesh=mesh, in_specs=in_specs, out_specs=out_specs, check_vma=False)
```

profile of v0, /device:TPU:15, one launch (start us, length us, event | category | flops | bytes accessed | tf_op | source)
XLA Modules:
  0.0 290.1 jit_solution(3233545299886751704)
XLA Ops:
  8.1 0.8 select_reduce_fusion
  9.6 1.0 scatter_custom_fusion
  11.3 4.5 %all-to-all-start = ((f32[8,1,32]{2,1,0:T(1,128)}), f32[8,1,32]{2,1,0:T(1,128)S(1)}, u32[]{:S(2)}, u32[]{:S(2)}) async-start(f32[8,1,32]{2,1,0:T(1,128)} %all_to_all.22), calls=%async_computation | async-start | bytes 8192 | tf_op jit(solution)/shard_map/all_to_all | solution.py:68
  16.4 11.8 %slice.36 = bf16[128,128,3,64]{3,1,2,0:T(8,128)(2,1)} slice(bf16[128,128,3,128]{3,1,2,0:T(8,128)(2,1)} %param.6), slice={[0:128], [0:128], [0:3], [64:128]} | slice | bytes 12582912 | tf_op jit(solution)/shard_map/slice | solution.py:12
  28.2 12.2 %copy.26 = bf16[128,128,3,64]{1,3,2,0:T(8,128)(2,1)} copy(bf16[128,128,3,64]{3,1,2,0:T(8,128)(2,1)} %slice.36) | data formatting | bytes 12582912
  40.5 4.4 %convert_element_type.34 = f32[128,128,3,64]{1,3,2,0:T(8,128)S(1)} convert(bf16[128,128,3,64]{1,3,2,0:T(8,128)(2,1)} %copy.26) | non-fusion elementwise | flops 3145728 | bytes 18874368 | tf_op jit(solution)/shard_map/convert_element_type | solution.py:12
  45.0 4.2 %multiply_convert_fusion.2 = (bf16[128,128,1,64]{1,3,2,0:T(8,128)(2,1)S(1)}, bf16[128,128,1,64]{1,3,2,0:T(8,128)(2,1)}, bf16[128,128,1,64]{1,3,2,0:T(8,128)(2,1)}) fusion(f32[128,128,3,64]{1,3,2,0:T(8,128)S(1)} %convert_element_type.34, f32[128,128]{1,0:T(8,128)S(1)} %get-tuple-element.15, f32[128,128]{1,0:T(8,128)S(1)} %get-tuple-element.16, ...), kind=kLoop, calls=%fused_computation.15 | loop fusion | flops 22020096 | bytes 19333120 | tf_op jit(solution)/shard_map/convert
  49.3 1.1 gather_fusion
  50.4 4.2 %all-to-all-start.1 = ((f32[8,1,32]{2,1,0:T(1,128)}), f32[8,1,32]{2,1,0:T(1,128)S(1)}, u32[]{:S(2)}, u32[]{:S(2)}) async-start(f32[8,1,32]{2,1,0:T(1,128)} %bitcast.5), calls=%async_computation.1 | async-start | bytes 8192 | tf_op jit(solution)/shard_map/all_to_all | solution.py:69
  54.6 10.3 %fusion.7 = f32[128,64,64]{1,2,0:T(8,128)} fusion(bf16[128,128,3,128]{3,1,2,0:T(8,128)(2,1)} %param.6, bf16[128,128,1,64]{1,3,2,0:T(8,128)(2,1)} %get-tuple-element.11, bf16[128,128,1,64]{1,3,2,0:T(8,128)(2,1)} %get-tuple-element.10, bf16[128,128,1,64]{1,3,2,0:T(8,128)(2,1)S(1)} %get-tuple-element.9), kind=kOutput, calls=%fused_computation.16 | convolution fusion | flops 408944640 | bytes 20971520 | tf_op jit(solution)/shard_map/spci,spcj->sij/dot_general | solution.py:39
  65.0 4.5 %copy.22 = f32[128,64,64]{0,2,1:T(8,128)S(1)} copy(f32[128,64,64]{1,2,0:T(8,128)} %fusion.7) | data formatting | bytes 4194304 | tf_op jit(solution)/shard_map/spci,spcj->sij/dot_general | solution.py:39
  69.5 1.9 copy.23
  71.3 5.0 %scatter_custom_fusion.1 = f32[256,4096]{1,0:T(8,128)} fusion(s32[128]{0:T(128)S(1)} %fusion.26, f32[128,4096]{1,0:T(8,128)} %copy.23, f32[]{:T(128)} %constant.6.clone.1), kind=kCustom, calls=%fused_computation.19 | custom fusion | bytes 4194816 | tf_op jit(solution)/shard_map/scatter | solution.py:55
  76.3 4.7 %all-to-all-start.2 = ((f32[8,32,4096]{2,1,0:T(8,128)}), f32[8,32,4096]{2,1,0:T(8,128)}, u32[]{:S(2)}, u32[]{:S(2)}) async-start(f32[8,32,4096]{2,1,0:T(8,128)} %bitcast.102), calls=%async_computation.2 | async-start | bytes 8388608 | tf_op jit(solution)/shard_map/all_to_all | solution.py:66
  81.0 5.0 %gather_fusion.1 = f32[8,32,4096]{2,1,0:T(8,128)} fusion(f32[8,32,4096]{2,1,0:T(8,128)} %bitcast.103, s32[1024]{0:T(1024)S(1)} %pad_clamp_fusion), kind=kCustom, calls=%fused_computation.1 | custom fusion | bytes 8388640 | tf_op jit(solution)/shard_map/gather | solution.py:63
  86.1 7.9 %reshape.265 = f32[8,32,64,64]{3,2,1,0:T(8,128)} reshape(f32[8,32,4096]{2,1,0:T(8,128)} %gather_fusion.1) | data formatting | bytes 8388608 | tf_op jit(solution)/shard_map/reshape | solution.py:63
  93.9 8.9 %copy.24 = f32[8,32,64,64]{3,2,1,0:T(8,128)} copy(f32[8,32,64,64]{2,3,1,0:T(8,128)} %bitcast.104) | data formatting | bytes 8388608 | tf_op jit(solution)/shard_map/transpose | solution.py:63
  102.8 7.9 %reshape.266 = f32[8,32,4096]{2,1,0:T(8,128)} reshape(f32[8,32,64,64]{3,2,1,0:T(8,128)} %copy.24) | data formatting | bytes 8388608 | tf_op jit(solution)/shard_map/reshape | solution.py:64
  110.7 16.8 %all-to-all-done.2 = f32[8,32,4096]{2,1,0:T(8,128)} async-done(((f32[8,32,4096]{2,1,0:T(8,128)}), f32[8,32,4096]{2,1,0:T(8,128)}, u32[]{:S(2)}, u32[]{:S(2)}) %all-to-all-start.2) | async-done | bytes 4194336 | tf_op jit(solution)/shard_map/all_to_all | solution.py:66
  127.5 7.2 %all-to-all-start.3 = ((f32[8,32,4096]{2,1,0:T(8,128)}), f32[8,32,4096]{2,1,0:T(8,128)}, u32[]{:S(2)}, u32[]{:S(2)}) async-start(f32[8,32,4096]{2,1,0:T(8,128)} %reshape.266), calls=%async_computation.3 | async-start | bytes 8388608 | tf_op jit(solution)/shard_map/all_to_all | solution.py:67
  134.8 46.4 %all-to-all-done.3 = f32[8,32,4096]{2,1,0:T(8,128)} async-done(((f32[8,32,4096]{2,1,0:T(8,128)}), f32[8,32,4096]{2,1,0:T(8,128)}, u32[]{:S(2)}, u32[]{:S(2)}) %all-to-all-start.3) | async-done | bytes 4194336 | tf_op jit(solution)/shard_map/all_to_all | solution.py:67
  181.2 7.7 %pad_maximum_fusion = f32[16,32,4096]{2,1,0:T(8,128)} fusion(f32[8,32,4096]{2,1,0:T(8,128)} %all-to-all-done.3, f32[8,32,4096]{2,1,0:T(8,128)} %all-to-all-done.2), kind=kLoop, calls=%fused_computation.7 | loop fusion | flops 2097152 | bytes 16777216 | tf_op jit(solution)/shard_map/concatenate | solution.py:71
  188.9 16.1 %scatter_custom_fusion.2 = f32[256,4096]{1,0:T(8,128)} fusion(s32[512]{0:T(512)S(1)} %reshape.302, f32[512,4096]{1,0:T(8,128)} %bitcast.106, f32[]{:T(128)} %constant.6.clone.1), kind=kCustom, calls=%fused_computation.17 | custom fusion | flops 2097152 | bytes 4194816 | tf_op jit(solution)/shard_map/scatter-add | solution.py:73
  205.1 78.2 %reduce-scatter.2.cloned.1.call-done = f32[64,4096]{1,0:T(8,128)} async-done(((f32[256,4096]{1,0:T(8,128)}), f32[64,4096]{1,0:T(8,128)}) %reduce-scatter.2.cloned.1.call-update) | async-done | bytes 1048592 | tf_op jit(solution)/shard_map/reduce_scatter | solution.py:74
  (19 shorter events, 3.8 us)
Async XLA Ops:
  11.3 39.2 %all-to-all-start = ((f32[8,1,32]{2,1,0:T(1,128)}), f32[8,1,32]{2,1,0:T(1,128)S(1)}, u32[]{:S(2)}, u32[]{:S(2)}) async-start(f32[8,1,32]{2,1,0:T(1,128)} %all_to_all.22), calls=%async_computation | async-start | bytes 8192 | tf_op jit(solution)/shard_map/all_to_all | solution.py:68
  40.5 4.4 %copy-start = (f32[128,6,128]{2,0,1:T(8,128)S(1)}, f32[128,6,128]{2,0,1:T(8,128)}, u32[]{:S(2)}) copy-start(f32[128,6,128]{2,0,1:T(8,128)} %param.7) | copy-start | bytes 1179652
  40.5 4.4 %copy-start.1 = (s32[1,128]{1,0:T(1,128)S(1)}, s32[1,128]{1,0:T(1,128)}, u32[]{:S(2)}) copy-start(s32[1,128]{1,0:T(1,128)} %param.8) | copy-start | bytes 1540
  50.4 25.9 %all-to-all-start.1 = ((f32[8,1,32]{2,1,0:T(1,128)}), f32[8,1,32]{2,1,0:T(1,128)S(1)}, u32[]{:S(2)}, u32[]{:S(2)}) async-start(f32[8,1,32]{2,1,0:T(1,128)} %bitcast.5), calls=%async_computation.1 | async-start | bytes 8192 | tf_op jit(solution)/shard_map/all_to_all | solution.py:69
  76.3 51.2 %all-to-all-start.2 = ((f32[8,32,4096]{2,1,0:T(8,128)}), f32[8,32,4096]{2,1,0:T(8,128)}, u32[]{:S(2)}, u32[]{:S(2)}) async-start(f32[8,32,4096]{2,1,0:T(8,128)} %bitcast.102), calls=%async_computation.2 | async-start | bytes 8388608 | tf_op jit(solution)/shard_map/all_to_all | solution.py:66
  127.5 53.7 %all-to-all-start.3 = ((f32[8,32,4096]{2,1,0:T(8,128)}), f32[8,32,4096]{2,1,0:T(8,128)}, u32[]{:S(2)}, u32[]{:S(2)}) async-start(f32[8,32,4096]{2,1,0:T(8,128)} %reshape.266), calls=%async_computation.3 | async-start | bytes 8388608 | tf_op jit(solution)/shard_map/all_to_all | solution.py:67
  134.7 148.5 %reduce-scatter.2.cloned.1.call-start = ((), (), s32[]{:S(2)}) async-start(), calls=%async_computation.5 | async-start | bytes 5242880 | tf_op jit(solution)/shard_map/reduce_scatter | solution.py:74
Sparse Core Ops, SparseCore 0:
  205.2 77.9 reduce-scatter.1
where the time goes:
time: 293 us; the launch traced here: 290 us
  waiting for transfers between devices  141 us (48%)
  local copies, waits for them, and re-layouts  68 us (23%)
  other arithmetic  36.2 us (12%)
  starting transfers between devices  20.6 us (7%)
  between operations  13.5 us (5%)
  matrix products  10.3 us (4%)
    reduce_scatter x1, waiting for transfers between devices, local(): lax.psum_scatter(dense_sums, 'tile', scatter_dimension=0, tiled=True)  78.2 us
    all_to_all x1, waiting for transfers between devices, local(): lax.all_to_all(flipped, 'orbit', split_axis=0, concat_axis=0, tiled=True)  46.4 us
    all_to_all x1, waiting for transfers between devices, local(): lax.all_to_all(outgoing, 'orbit', split_axis=0, concat_axis=0, tiled=True)  16.8 us
    scatter-add x1, other arithmetic, local(): dense_sums = jax.ops.segment_sum(gathered, pair_tags, num_segments=PAIR_ORB)  16.1 us
    unnamed x5, local copies, waits for them, and re-layouts  12.2 us
    slice x1, local copies, waits for them, and re-layouts, eliminate(): right_half = jacobians[..., params:].astype(jnp.float32)  11.8 us
    dot_general x1, matrix products, eliminate(): jnp.einsum('spci,spcj->sij', left_half, solved, preferred_element_type=jn...  10.3 us
    transpose x1, local copies, waits for them, and re-layouts, local(): jnp.swapaxes(outgoing[crossing].reshape(orbits, capacity, params, params)...  8.92 us
  transfers between devices with their start and end apart: 5, of which 3 were waited for; matrix products, arithmetic and copies ran while one was open for 30% of the time, Pallas kernels for 0%

commit v1 on v0

v1 whole, which is shorter than its diff:
```python
import functools

import jax
import jax.numpy as jnp
from jax import lax
from jax.experimental import pallas as pl
from jax.experimental.pallas import tpu as pltpu
from jax.sharding import PartitionSpec as P

PAIR_ORB = 256
LANES = 128


def weights(normals, counts):
    d1, d2, d3, ab, ac, bc = (normals[i] for i in range(6))
    cof_aa = d2 * d3 - bc * bc
    cof_bb = d1 * d3 - ac * ac
    cof_cc = d1 * d2 - ab * ab
    cof_ab = ac * bc - ab * d3
    cof_ac = ab * bc - ac * d2
    cof_bc = ab * ac - d1 * bc
    det = d1 * cof_aa + ab * cof_ab + ac * cof_ac
    places = lax.broadcasted_iota(jnp.int32, det.shape, 1)
    scale = jnp.where(places < counts, 1.0, 0.0) / det
    rows = ((cof_aa, cof_ab, cof_ac), (cof_ab, cof_bb, cof_bc), (cof_ac, cof_bc, cof_cc))
    return [[entry * scale for entry in row] for row in rows]


def slot_block(jac, coef, s, flip):
    params = jac.shape[-1] // 2
    points = jac.shape[-2]
    right = [jnp.transpose(jac[e])[params:].astype(jnp.float32) for e in range(3)]
    solved = [
        (coef[c][0][s : s + 1] * right[0] + coef[c][1][s : s + 1] * right[1] + coef[c][2][s : s + 1] * right[2]).astype(jnp.bfloat16)
        for c in range(3)
    ]
    mirrored = jnp.dot(
        jnp.concatenate(solved, axis=1), jac.reshape(3 * points, 2 * params), preferred_element_type=jnp.float32
    )
    straight = jnp.transpose(mirrored)[:params]
    return jnp.where(flip > 0, mirrored[:, :params], straight)


def blocks_kernel(jac_ref, normals_ref, counts_ref, flip_ref, out_ref, scratch):
    slots, params = jac_ref.shape[0], jac_ref.shape[3] // 2
    chunks, _, width = out_ref.shape
    coef = weights(normals_ref[...], counts_ref[...])
    for s in range(slots):
        scratch[s * params : (s + 1) * params, :] = slot_block(jac_ref[s], coef, s, flip_ref[s : s + 1, :params])
    for tile in range(chunks * width // LANES):
        pieces = [scratch[pl.ds(2 * tile + half, slots, stride=params), :] for half in range(2)]
        c, at = divmod(tile * LANES, width)
        out_ref[c, :, at : at + LANES] = jnp.concatenate(pieces, axis=1)


def oriented_blocks(jac, normals, counts, flip, chunks):
    slots, _, points, both = jac.shape
    params = both // 2
    width = params * params // chunks
    step = min(16, slots)
    return pl.pallas_call(
        blocks_kernel,
        grid=(slots // step,),
        in_specs=[
            pl.BlockSpec((step, 3, points, both), lambda g: (g, 0, 0, 0)),
            pl.BlockSpec((6, step, points), lambda g: (0, g, 0)),
            pl.BlockSpec((step, points), lambda g: (g, 0)),
            pl.BlockSpec((step, points), lambda g: (g, 0)),
        ],
        out_specs=pl.BlockSpec((chunks, step, width), lambda g: (0, g, 0)),
        out_shape=jax.ShapeDtypeStruct((chunks, slots, width), jnp.float32),
        scratch_shapes=[pltpu.VMEM((step * params, params), jnp.float32)],
        compiler_params=pltpu.CompilerParams(vmem_limit_bytes=32 * 1024 * 1024),
    )(jac, normals, counts, flip)


def local(jacobians, point_normals, block_counts, pair_owner, pair_local, crossing):
    slots, points, _, both = jacobians.shape
    params = both // 2
    orbits, tiles = lax.axis_size("orbit"), lax.axis_size("tile")
    couples, share = orbits // 2, PAIR_ORB // tiles
    jac = jnp.transpose(jacobians, (0, 2, 1, 3))
    normals = jnp.transpose(point_normals, (1, 0, 2))
    counts = jnp.broadcast_to(block_counts[0][:, None], (slots, points))
    orbit_ids = jnp.arange(orbits, dtype=jnp.int32)
    leads = orbit_ids < crossing
    couple = jnp.sum((orbit_ids[None, :] < jnp.minimum(orbit_ids, crossing)[:, None]) & leads[None, :], axis=1).astype(jnp.int32)
    owner_hot = pair_owner == orbit_ids[None, :]
    slot_couple = jnp.sum(jnp.where(owner_hot, couple[None, :], 0), axis=1)
    flip = jnp.sum(jnp.where(owner_hot & ~leads[None, :], 1, 0), axis=1)
    flip = jnp.broadcast_to(flip[:, None], (slots, points))
    row = (pair_local // share) * (couples * share) + slot_couple * share + pair_local % share

    blocks = oriented_blocks(jac, normals, counts, flip, orbits)
    arrived = lax.all_to_all(blocks, "orbit", split_axis=0, concat_axis=0, tiled=True).reshape(orbits * slots, -1)
    rows = lax.all_gather(row, "orbit", tiled=True)
    hot = (jnp.arange(couples * PAIR_ORB, dtype=jnp.int32)[:, None] == rows[None, :]).astype(jnp.bfloat16)
    high = lax.reduce_precision(arrived, 8, 7)
    low = arrived - high
    dense = jnp.dot(hot, high.astype(jnp.bfloat16), preferred_element_type=jnp.float32) + jnp.dot(
        hot, low.astype(jnp.bfloat16), preferred_element_type=jnp.float32
    )
    owned = lax.psum_scatter(dense, "tile", scatter_dimension=0, tiled=True)
    owned = owned.reshape(couples, share, -1)[couple]
    parts = lax.all_to_all(owned, "orbit", split_axis=0, concat_axis=0, tiled=True)
    whole = jnp.transpose(parts, (1, 0, 2)).reshape(share, params, params)
    mine = leads[lax.axis_index("orbit")]
    whole = jnp.where(mine, whole, jnp.swapaxes(whole, 1, 2))
    return whole.reshape(1, share, params * params)


def solution(mesh):
    in_specs = (
        P(("tile", "orbit"), None, None, None),
        P(("tile", "orbit"), None, None),
        P(("tile", "orbit"), None),
        P(("tile", "orbit"), None),
        P(("tile", "orbit")),
        P(),
    )
    out_specs = P("orbit", "tile", None)
    return jax.shard_map(local, mesh=mesh, in_specs=in_specs, out_specs=out_specs, check_vma=False)
```

time: 293 us -> 154 us (0.53)
  the two profiles are of different devices: /device:TPU:15 before, /device:TPU:0 now
where the time goes in v1:
time: 154 us
  waiting for transfers between devices  58.2 us (38%)
  blocking collectives  29.5 us (19%)
  Pallas kernels  17.9 us (12%)
  local copies, waits for them, and re-layouts  15.4 us (10%)
  between operations  13.5 us (9%)
  starting transfers between devices  8.99 us (6%)
  other arithmetic  6.53 us (4%)
  matrix products  3.86 us (3%)
    reduce_scatter x1, waiting for transfers between devices, local(): owned = lax.psum_scatter(dense, 'tile', scatter_dimension=0, tiled=True)  43.4 us
    all_gather x1, blocking collectives, local(): rows = lax.all_gather(row, 'orbit', tiled=True)  29.5 us
    pallas_call x1, Pallas kernels, oriented_blocks(): pl.pallas_call(blocks_kernel, grid=(slots // step,), in_specs=[pl.BlockSp...  17.9 us
    all_to_all x1, waiting for transfers between devices, local(): lax.all_to_all(owned, 'orbit', split_axis=0, concat_axis=0, tiled=True)  14.8 us
    unnamed x6, local copies, waits for them, and re-layouts  5.58 us
    all_to_all x1, starting transfers between devices, local(): lax.all_to_all(blocks, 'orbit', split_axis=0, concat_axis=0, tiled=True)  5.3 us
    select_n x1, other arithmetic, local(): whole = jnp.where(mine, whole, jnp.swapaxes(whole, 1, 2))  3.94 us
    all_to_all x1, starting transfers between devices, local(): lax.all_to_all(owned, 'orbit', split_axis=0, concat_axis=0, tiled=True)  3.65 us
  transfers between devices with their start and end apart: 3, of which 2 were waited for; matrix products, arithmetic and copies ran while one was open for 0% of the time, Pallas kernels for 0%

profile of v1, /device:TPU:0, one launch (start us, length us, event | category | flops | bytes accessed | tf_op | source)
XLA Modules:
  0.0 153.9 jit_solution(4406549943459169589)
XLA Ops:
  6.5 0.7 fusion.11
  7.2 0.7 iota_minimum_fusion
  7.9 0.2 convert_reduce_fusion
  8.0 0.7 select_reduce_fusion.1
  8.8 0.1 broadcast_in_dim.45.flip_ref
  8.9 0.7 broadcast_in_dim.27.counts_ref
  9.6 4.6 %copy-done = bf16[128,128,3,128]{3,1,2,0:T(8,128)(2,1)S(1)} copy-done((bf16[128,128,3,128]{3,1,2,0:T(8,128)(2,1)S(1)}, bf16[128,128,3,128]{3,1,2,0:T(8,128)(2,1)}, u32[]{:S(2)}) %copy-start) | copy-done | bytes 12582936
  14.2 1.0 copy-done.1
  15.2 17.9 %shard_map.64 = f32[8,128,512]{2,1,0:T(8,128)} custom-call(bf16[128,3,128,128]{3,2,1,0:T(8,128)(2,1)S(1)} %bitcast.21, f32[6,128,128]{2,1,0:T(8,128)S(1)} %bitcast.22, s32[128,128]{1,0:T(8,128)S(1)} %broadcast_in_dim.27.counts_ref, s32[128,128]{1,0:T(8,128)S(1)} %broadcast_in_dim.45.flip_ref), custom_call_target="tpu_custom_call" | custom-call | tf_op jit(solution)/shard_map/pallas_call | solution.py:61
  33.1 5.3 %all-to-all-start = ((f32[8,128,512]{2,1,0:T(8,128)}), f32[8,128,512]{2,1,0:T(8,128)S(1)}, u32[]{:S(2)}, u32[]{:S(2)}) async-start(f32[8,128,512]{2,1,0:T(8,128)} %shard_map.64), calls=%async_computation | async-start | bytes 4194304 | tf_op jit(solution)/shard_map/all_to_all | solution.py:95
  38.5 29.5 %all-gather = s32[8,1,128]{2,1,0:T(1,128)S(1)} all-gather(s32[1,1,128]{2,1,0:T(1,128)S(1)} %fusion.10), channel_id=1, replica_groups=mesh['tile'=4,'orbit'=8] {'orbit'}, dimensions={0}, use_global_device_ids=true | all-gather | bytes 4608 | tf_op jit(solution)/shard_map/all_gather | solution.py:96
  68.0 0.3 reduce-precision_convert_fusion
  68.3 1.3 fusion
  69.6 2.6 %fusion.5 = f32[1024,512]{1,0:T(8,128)} fusion(f32[1024,512]{1,0:T(8,128)S(1)} %fusion, bf16[1024,512]{1,0:T(8,128)(2,1)S(1)} %get-tuple-element.7, s32[1024]{0:T(1024)S(1)} %bitcast.26), kind=kOutput, calls=%fused_computation.10 | convolution fusion | flops 1075314688 | bytes 5246976 | tf_op jit(solution)/shard_map/dot_general | solution.py:100
  72.3 43.4 %reduce-scatter.2.cloned.1.call-done = f32[256,512]{1,0:T(8,128)} async-done(((f32[1024,512]{1,0:T(8,128)}), f32[256,512]{1,0:T(8,128)}) %reduce-scatter.2.cloned.1.call-update) | async-done | bytes 524304 | tf_op jit(solution)/shard_map/reduce_scatter | solution.py:103
  115.7 2.6 %gather_fusion = f32[8,64,512]{2,1,0:T(8,128)} fusion(f32[4,64,512]{2,1,0:T(8,128)} %bitcast.24, s32[1024]{0:T(1024)S(1)} %pad_clamp_fusion), kind=kCustom, calls=%fused_computation | custom fusion | bytes 2097184 | tf_op jit(solution)/shard_map/gather | solution.py:104
  118.3 3.7 %all-to-all-start.1 = ((f32[8,64,512]{2,1,0:T(8,128)}), f32[8,64,512]{2,1,0:T(8,128)S(1)}, u32[]{:S(2)}, u32[]{:S(2)}) async-start(f32[8,64,512]{2,1,0:T(8,128)} %gather_fusion), calls=%async_computation.2 | async-start | bytes 2097152 | tf_op jit(solution)/shard_map/all_to_all | solution.py:105
  121.9 0.6 dynamic_slice.3
  122.5 14.8 %all-to-all-done.1 = f32[8,64,512]{2,1,0:T(8,128)S(1)} async-done(((f32[8,64,512]{2,1,0:T(8,128)}), f32[8,64,512]{2,1,0:T(8,128)S(1)}, u32[]{:S(2)}, u32[]{:S(2)}) %all-to-all-start.1) | async-done | bytes 1048608 | tf_op jit(solution)/shard_map/all_to_all | solution.py:105
  137.3 0.6 copy.13
  138.0 0.4 reshape.35
  138.4 1.9 %copy.14 = f32[64,64,64]{1,2,0:T(8,128)} copy(f32[64,64,64]{2,1,0:T(8,128)S(1)} %reshape.35) | data formatting | bytes 2097152 | tf_op jit(solution)/shard_map/reshape | solution.py:106
  140.2 3.9 %bitcast_select_fusion = f32[64,64,64]{2,1,0:T(8,128)} fusion(f32[64,64,64]{2,1,0:T(8,128)S(1)} %reshape.35, f32[64,64,64]{1,2,0:T(8,128)} %copy.14, pred[]{:T(512)} %bitcast), kind=kLoop, calls=%fused_computation.7 | loop fusion | flops 262144 | bytes 3145729 | tf_op jit(solution)/shard_map/jit(_where)/select_n | solution.py:108
  144.2 2.9 %reshape.36 = f32[1,64,4096]{2,1,0:T(8,128)} reshape(f32[64,64,64]{2,1,0:T(8,128)} %bitcast_select_fusion) | data formatting | bytes 2097152 | tf_op jit(solution)/shard_map/reshape | solution.py:109
  (10 shorter events, 0.1 us)
Async XLA Ops:
  9.6 4.6 %copy-start = (bf16[128,128,3,128]{3,1,2,0:T(8,128)(2,1)S(1)}, bf16[128,128,3,128]{3,1,2,0:T(8,128)(2,1)}, u32[]{:S(2)}) copy-start(bf16[128,128,3,128]{3,1,2,0:T(8,128)(2,1)} %param.6) | copy-start | bytes 37748740
  14.2 1.0 copy-start.1
  33.1 5.3 %copy-start.2 = (s32[128]{0:T(128)S(1)}, s32[128]{0:T(128)}, u32[]{:S(2)}) copy-start(s32[128]{0:T(128)} %param.10) | copy-start | bytes 1540
  33.1 34.9 %all-to-all-start = ((f32[8,128,512]{2,1,0:T(8,128)}), f32[8,128,512]{2,1,0:T(8,128)S(1)}, u32[]{:S(2)}, u32[]{:S(2)}) async-start(f32[8,128,512]{2,1,0:T(8,128)} %shard_map.64), calls=%async_computation | async-start | bytes 4194304 | tf_op jit(solution)/shard_map/all_to_all | solution.py:95
  38.4 77.2 %reduce-scatter.2.cloned.1.call-start = ((), (), s32[]{:S(2)}) async-start(), calls=%async_computation.3 | async-start | bytes 2621440 | tf_op jit(solution)/shard_map/reduce_scatter | solution.py:103
  118.3 19.1 %all-to-all-start.1 = ((f32[8,64,512]{2,1,0:T(8,128)}), f32[8,64,512]{2,1,0:T(8,128)S(1)}, u32[]{:S(2)}, u32[]{:S(2)}) async-start(f32[8,64,512]{2,1,0:T(8,128)} %gather_fusion), calls=%async_computation.2 | async-start | bytes 2097152 | tf_op jit(solution)/shard_map/all_to_all | solution.py:105
Sparse Core Ops, SparseCore 0:
  72.4 43.2 reduce-scatter.1

commit v2 on v1

v2 whole, which is shorter than its diff:
```python
import jax
import jax.numpy as jnp
from jax import lax
from jax.experimental import pallas as pl
from jax.experimental.pallas import tpu as pltpu
from jax.sharding import PartitionSpec as P

PAIR_ORB = 256
LANES = 128
MESH = pl.DeviceIdType.MESH


def weights(normals, counts):
    d1, d2, d3, ab, ac, bc = (normals[i] for i in range(6))
    cof_aa = d2 * d3 - bc * bc
    cof_bb = d1 * d3 - ac * ac
    cof_cc = d1 * d2 - ab * ab
    cof_ab = ac * bc - ab * d3
    cof_ac = ab * bc - ac * d2
    cof_bc = ab * ac - d1 * bc
    det = d1 * cof_aa + ab * cof_ab + ac * cof_ac
    places = lax.broadcasted_iota(jnp.int32, det.shape, 1)
    scale = jnp.where(places < counts, 1.0, 0.0) / det
    rows = ((cof_aa, cof_ab, cof_ac), (cof_ab, cof_bb, cof_bc), (cof_ac, cof_bc, cof_cc))
    return [[entry * scale for entry in row] for row in rows]


def slot_block(jac, coef, s, flip):
    params = jac.shape[-1] // 2
    points = jac.shape[-2]
    right = [jnp.transpose(jac[e])[params:].astype(jnp.float32) for e in range(3)]
    solved = [
        (coef[c][0][s : s + 1] * right[0] + coef[c][1][s : s + 1] * right[1] + coef[c][2][s : s + 1] * right[2]).astype(jnp.bfloat16)
        for c in range(3)
    ]
    mirrored = jnp.dot(
        jnp.concatenate(solved, axis=1), jac.reshape(3 * points, 2 * params), preferred_element_type=jnp.float32
    )
    straight = jnp.transpose(mirrored)[:params]
    return jnp.where(flip > 0, mirrored[:, :params], straight)


def each(low, high, body):
    def step(i, carry):
        body(i)
        return carry

    lax.fori_loop(low, high, step, 0)


def reduce_kernel(
    jac_hbm, normals_ref, counts_ref, flip_ref, ids_ref, couple_ref, fin_ref,
    jac_v, send, arrived, ids_all, hot, halves, dense, passing, stage, scratch,
    jac_sem, ids_ssem, ids_rsem, a_ssem, a_rsem, b_ssem, b_rsem, c_ssem, c_rsem, own_sem,
):
    groups, orbits, tiles = jac_sem.shape[0], arrived.shape[0], dense.shape[0]
    units, share, rank = fin_ref.shape[1], fin_ref.shape[2], dense.shape[2]
    slots, params = jac_v.shape[0], jac_v.shape[3] // 2
    step, half_rows = slots // groups, params // 2
    t, o = lax.axis_index("tile"), lax.axis_index("orbit")

    def peer_of(k):
        return lax.rem(o + k, orbits)

    def jac_copy(g):
        rows = pl.ds(pl.multiple_of(g * step, step), step)
        return pltpu.make_async_copy(jac_hbm.at[rows], jac_v.at[rows], jac_sem.at[g])

    def ids_copy(peer, src):
        return pltpu.make_async_remote_copy(
            src_ref=ids_ref, dst_ref=ids_all.at[src], send_sem=ids_ssem.at[peer], recv_sem=ids_rsem.at[src],
            device_id=(t, peer), device_id_type=MESH)

    def block_copy(peer, src, g):
        rows = pl.ds(pl.multiple_of(g * step, step), step)
        return pltpu.make_async_remote_copy(
            src_ref=send.at[peer, rows], dst_ref=arrived.at[src, rows], send_sem=a_ssem.at[peer, g],
            recv_sem=a_rsem.at[src, g], device_id=(t, peer), device_id_type=MESH)

    def sum_copy(side, d, u, to):
        return pltpu.make_async_remote_copy(
            src_ref=dense.at[d, u], dst_ref=passing.at[side, d, u], send_sem=b_ssem.at[d, u],
            recv_sem=b_rsem.at[side, d, u], device_id=(to, o), device_id_type=MESH)

    def out_copy(peer, src, u):
        return pltpu.make_async_remote_copy(
            src_ref=stage.at[peer, u], dst_ref=fin_ref.at[src, u], send_sem=c_ssem.at[peer, u],
            recv_sem=c_rsem.at[src, u], device_id=(t, peer), device_id_type=MESH)

    each(0, groups, lambda g: jac_copy(g).start())
    barrier = pltpu.get_barrier_semaphore()
    each(1, orbits, lambda k: pl.semaphore_signal(barrier, inc=1, device_id=(t, peer_of(k)), device_id_type=MESH))

    @pl.when(t > 0)
    def _():
        pl.semaphore_signal(barrier, inc=1, device_id=(t - 1, o), device_id_type=MESH)

    @pl.when(t < tiles - 1)
    def _():
        pl.semaphore_signal(barrier, inc=1, device_id=(t + 1, o), device_id_type=MESH)

    ends = (t == 0).astype(jnp.int32) + (t == tiles - 1).astype(jnp.int32)
    pl.semaphore_wait(barrier, orbits + 1 - ends)
    each(1, orbits, lambda k: ids_copy(peer_of(k), o).start())
    ids_all[o] = ids_ref[...]

    def group(g):
        jac_copy(g).wait()
        at = pl.multiple_of(g * step, step)
        rows = pl.ds(at, step)
        coef = weights(normals_ref[:, rows, :], counts_ref[rows, :])
        flips = flip_ref[rows, :]
        for s in range(step):
            scratch[s * params : (s + 1) * params, :] = slot_block(jac_v[at + s], coef, s, flips[s : s + 1, :params])
        for unit in range(orbits * units):
            pieces = [scratch[pl.ds(unit + half * half_rows, step, stride=params), :] for half in range(2)]
            c, u = divmod(unit, units)
            send[c, rows, u * LANES : (u + 1) * LANES] = jnp.concatenate(pieces, axis=1)
        arrived[o, rows, :] = send[o, rows, :]
        each(1, orbits, lambda k: block_copy(peer_of(k), o, g).start())

    each(0, groups, group)

    each(1, orbits, lambda k: ids_copy(peer_of(k), peer_of(k)).wait_recv())

    def fill_hot(d):
        want = lax.broadcasted_iota(jnp.int32, (rank, slots), 0) + d * rank
        for p in range(orbits):
            hot[d, :, p * slots : (p + 1) * slots] = jnp.where(want == ids_all[p, 0:1, :], 1.0, 0.0).astype(jnp.bfloat16)

    each(0, tiles, fill_hot)
    each(1, orbits, lambda k: each(0, groups, lambda g: block_copy(peer_of(k), peer_of(k), g).wait_recv()))

    for u in range(units):
        found = arrived[:, :, u * LANES : (u + 1) * LANES].reshape(orbits * slots, LANES)
        high = found.astype(jnp.bfloat16)
        low = (found - high.astype(jnp.float32)).astype(jnp.bfloat16)
        halves[:, :LANES] = high
        halves[:, LANES:] = low

        def add_up(d):
            both = jnp.dot(hot[d], halves[...], preferred_element_type=jnp.float32)
            dense[d, u] = both[:, :LANES] + both[:, LANES:]

        each(0, tiles, add_up)

        @pl.when(t == 0)
        def _():
            each(1, tiles, lambda i: sum_copy(0, tiles - i, u, 1).start())

        @pl.when(t == tiles - 1)
        def _():
            each(0, tiles - 1, lambda d: sum_copy(1, d, u, tiles - 2).start())

    def finish(u):
        def relay(i):
            d = tiles - 1 - i

            @pl.when((t > 0) & (t < d))
            def _():
                sum_copy(0, d, u, t + 1).wait_recv()
                dense[d, u] = dense[d, u] + passing[0, d, u]
                sum_copy(0, d, u, t + 1).start()

            @pl.when((t < tiles - 1) & (t > i))
            def _():
                sum_copy(1, i, u, t - 1).wait_recv()
                dense[i, u] = dense[i, u] + passing[1, i, u]
                sum_copy(1, i, u, t - 1).start()

        each(0, tiles, relay)

        @pl.when(t > 0)
        def _():
            sum_copy(0, t, u, t - 1).wait_recv()
            dense[t, u] = dense[t, u] + passing[0, t, u]

        @pl.when(t < tiles - 1)
        def _():
            sum_copy(1, t, u, t + 1).wait_recv()
            dense[t, u] = dense[t, u] + passing[1, t, u]

        def hand_out(k):
            peer = peer_of(k)
            wanted = couple_ref[peer][0:1, :]
            taken = dense[t, u, 0:share, :]
            for c in range(1, orbits // 2):
                taken = jnp.where(wanted == c, dense[t, u, c * share : (c + 1) * share, :], taken)
            stage[peer, u] = taken

        each(0, orbits, hand_out)
        each(1, orbits, lambda k: out_copy(peer_of(k), o, u).start())
        pltpu.make_async_copy(stage.at[o, u], fin_ref.at[o, u], own_sem.at[u]).start()

    each(0, units, finish)

    def settle(u):
        pltpu.make_async_copy(stage.at[o, u], fin_ref.at[o, u], own_sem.at[u]).wait()
        each(1, orbits, lambda k: out_copy(peer_of(k), peer_of(k), u).wait_recv())
        each(1, orbits, lambda k: out_copy(peer_of(k), o, u).wait_send())

        def sent(d):
            @pl.when(t != d)
            def _():
                sum_copy(0, d, u, 0).wait_send()

        each(0, tiles, sent)

    each(0, units, settle)
    each(1, orbits, lambda k: ids_copy(peer_of(k), o).wait_send())
    each(1, orbits, lambda k: each(0, groups, lambda g: block_copy(peer_of(k), o, g).wait_send()))


def reduced_parts(jac, normals, counts, flip, ids, couple, orbits, tiles):
    slots, _, points, both = jac.shape
    params = both // 2
    step = min(16, slots)
    groups = slots // step
    units = params * params // LANES // orbits
    share = PAIR_ORB // tiles
    rank = orbits // 2 * share
    vmem = pl.BlockSpec(memory_space=pltpu.VMEM)
    f32 = jnp.float32
    dma = pltpu.SemaphoreType.DMA
    return pl.pallas_call(
        reduce_kernel,
        in_specs=[pl.BlockSpec(memory_space=pl.ANY), vmem, vmem, vmem, vmem, vmem],
        out_specs=pl.BlockSpec(memory_space=pl.ANY),
        out_shape=jax.ShapeDtypeStruct((orbits, units, share, LANES), f32),
        scratch_shapes=[
            pltpu.VMEM(jac.shape, jac.dtype),
            pltpu.VMEM((orbits, slots, units * LANES), f32),
            pltpu.VMEM((orbits, slots, units * LANES), f32),
            pltpu.VMEM((orbits,) + ids.shape, jnp.int32),
            pltpu.VMEM((tiles, rank, orbits * slots), jnp.bfloat16),
            pltpu.VMEM((orbits * slots, 2 * LANES), jnp.bfloat16),
            pltpu.VMEM((tiles, units, rank, LANES), f32),
            pltpu.VMEM((2, tiles, units, rank, LANES), f32),
            pltpu.VMEM((orbits, units, share, LANES), f32),
            pltpu.VMEM((step * params, params), f32),
            dma((groups,)),
            dma((orbits,)),
            dma((orbits,)),
            dma((orbits, groups)),
            dma((orbits, groups)),
            dma((tiles, units)),
            dma((2, tiles, units)),
            dma((orbits, units)),
            dma((orbits, units)),
            dma((units,)),
        ],
        compiler_params=pltpu.CompilerParams(
            collective_id=0, has_side_effects=True, vmem_limit_bytes=48 * 1024 * 1024
        ),
    )(jac, normals, counts, flip, ids, couple)


def assemble_kernel(lead_ref, fin_ref, out_ref, turned):
    count, share, _ = fin_ref.shape
    params = 2 * count
    half = LANES // 2

    @pl.when(lead_ref[0] > 0)
    def _():
        for m in range(count):
            first = (2 * m) % count
            side = (2 * m) // count * half
            out_ref[:, m * LANES : (m + 1) * LANES] = jnp.concatenate(
                [fin_ref[first + i, :, side : side + half] for i in range(2)], axis=1
            )

    @pl.when(lead_ref[0] == 0)
    def _():
        for unit in range(count):
            turned[unit * LANES : (unit + 1) * LANES, :] = jnp.transpose(fin_ref[unit])
        for m in range(count):
            rows = [turned[pl.ds(2 * m + k + h * params, count, stride=LANES), :] for k in range(2) for h in range(2)]
            out_ref[:, m * LANES : (m + 1) * LANES] = jnp.transpose(jnp.concatenate(rows, axis=0))


def assembled(lead, fin):
    count, share, _ = fin.shape
    vmem = pl.BlockSpec(memory_space=pltpu.VMEM)
    return pl.pallas_call(
        assemble_kernel,
        in_specs=[pl.BlockSpec(memory_space=pltpu.SMEM), vmem],
        out_specs=vmem,
        out_shape=jax.ShapeDtypeStruct((share, count * LANES), jnp.float32),
        scratch_shapes=[pltpu.VMEM((count * LANES, share), jnp.float32)],
        compiler_params=pltpu.CompilerParams(vmem_limit_bytes=16 * 1024 * 1024),
    )(lead, fin)


def local(jacobians, point_normals, block_counts, pair_owner, pair_local, crossing):
    slots, points, _, both = jacobians.shape
    orbits, tiles = lax.axis_size("orbit"), lax.axis_size("tile")
    couples, share = orbits // 2, PAIR_ORB // tiles
    jac = jnp.transpose(jacobians, (0, 2, 1, 3))
    normals = jnp.transpose(point_normals, (1, 0, 2))
    counts = jnp.broadcast_to(block_counts[0][:, None], (slots, points))
    orbit_ids = jnp.arange(orbits, dtype=jnp.int32)
    leads = orbit_ids < crossing
    couple = jnp.sum((orbit_ids[None, :] < jnp.minimum(orbit_ids, crossing)[:, None]) & leads[None, :], axis=1).astype(jnp.int32)
    owner_hot = pair_owner == orbit_ids[None, :]
    slot_couple = jnp.sum(jnp.where(owner_hot, couple[None, :], 0), axis=1)
    flip = jnp.sum(jnp.where(owner_hot & ~leads[None, :], 1, 0), axis=1)
    flip = jnp.broadcast_to(flip[:, None], (slots, points))
    row = (pair_local // share) * (couples * share) + slot_couple * share + pair_local % share
    ids = jnp.broadcast_to(row[None, :], (8, slots))
    wanted = jnp.broadcast_to(couple[:, None, None], (orbits, 8, LANES))
    fin = reduced_parts(jac, normals, counts, flip, ids, wanted, orbits, tiles)
    lead = leads[lax.axis_index("orbit")].astype(jnp.int32).reshape(1)
    return assembled(lead, fin.reshape(-1, share, LANES))[None]


def solution(mesh):
    in_specs = (
        P(("tile", "orbit"), None, None, None),
        P(("tile", "orbit"), None, None),
        P(("tile", "orbit"), None),
        P(("tile", "orbit"), None),
        P(("tile", "orbit")),
        P(),
    )
    out_specs = P("orbit", "tile", None)
    return jax.shard_map(local, mesh=mesh, in_specs=in_specs, out_specs=out_specs, check_vma=False)
```

time: 154 us -> 95 us (0.62)
  the two profiles are of different devices: /device:TPU:0 before, /device:TPU:5 now
where the time goes in v2:
time: 95 us; the launch traced here: 94.8 us
  Pallas kernels  88.7 us (93%)
  other arithmetic  2.91 us (3%)
  local copies, waits for them, and re-layouts  2.48 us (3%)
    pallas_call x1, Pallas kernels, reduced_parts(): pl.pallas_call(reduce_kernel, in_specs=[pl.BlockSpec(memory_space=pl.ANY)...  86 us
    pallas_call x1, Pallas kernels, assembled(): pl.pallas_call(assemble_kernel, in_specs=[pl.BlockSpec(memory_space=pltpu...  2.78 us

profile of v2, /device:TPU:5, one launch (start us, length us, event | category | flops | bytes accessed | tf_op | source)
XLA Modules:
  0.0 94.8 jit_solution(6205599417157782350)
XLA Ops:
  0.0 0.7 iota_minimum_fusion
  0.7 0.7 fusion.3
  1.3 0.6 dynamic_slice.3
  2.6 0.2 convert_reduce_fusion
  2.7 0.7 select_reduce_fusion
  3.5 0.7 fusion.2
  4.2 0.1 broadcast_in_dim.59.couple_ref
  4.2 0.1 broadcast_in_dim.56.flip_ref
  4.3 0.7 broadcast_in_dim.31.counts_ref
  5.1 0.0 copy-start
  5.1 1.0 %copy-done = f32[128,6,128]{2,0,1:T(8,128)S(1)} copy-done((f32[128,6,128]{2,0,1:T(8,128)S(1)}, f32[128,6,128]{2,0,1:T(8,128)}, u32[]{:S(2)}) %copy-start) | copy-done | bytes 393240
  6.1 86.0 %shard_map.64 = f32[8,4,64,128]{3,2,1,0:T(8,128)S(1)} custom-call(bf16[128,3,128,128]{3,2,1,0:T(8,128)(2,1)} %bitcast.8, f32[6,128,128]{2,1,0:T(8,128)S(1)} %bitcast.7, s32[128,128]{1,0:T(8,128)S(1)} %broadcast_in_dim.31.counts_ref, s32[128,128]{1,0:T(8,128)S(1)} %broadcast_in_dim.56.flip_ref, s32[8,128]{1,0:T(8,128)S(1)} %broadcast_in_dim.58.ids_ref, ...), custom_call_target="tpu_custom_call" | custom-call | tf_op jit(solution)/shard_map/pallas_call | solution.py:225
  92.0 2.8 %shard_map.65 = f32[64,4096]{1,0:T(8,128)} custom-call(s32[1]{0:T(128)S(6)} %convert_element_type.7.lead_ref, f32[32,64,128]{2,1,0:T(8,128)S(1)} %bitcast.6), custom_call_target="tpu_custom_call" | custom-call | tf_op jit(solution)/shard_map/pallas_call | solution.py:284
  (1 shorter events, 0.0 us)
Async XLA Ops:
  5.1 1.0 %copy-start = (f32[128,6,128]{2,0,1:T(8,128)S(1)}, f32[128,6,128]{2,0,1:T(8,128)}, u32[]{:S(2)}) copy-start(f32[128,6,128]{2,0,1:T(8,128)} %param.7) | copy-start | bytes 1179652

commit v3 on v2

v3 whole, which is shorter than its diff:
```python
import jax
import jax.numpy as jnp
from jax import lax
from jax.experimental import pallas as pl
from jax.experimental.pallas import tpu as pltpu
from jax.sharding import PartitionSpec as P

PAIR_ORB = 256
LANES = 128
MESH = pl.DeviceIdType.MESH


def weights(normals, counts):
    d1, d2, d3, ab, ac, bc = (normals[i] for i in range(6))
    cof_aa = d2 * d3 - bc * bc
    cof_bb = d1 * d3 - ac * ac
    cof_cc = d1 * d2 - ab * ab
    cof_ab = ac * bc - ab * d3
    cof_ac = ab * bc - ac * d2
    cof_bc = ab * ac - d1 * bc
    det = d1 * cof_aa + ab * cof_ab + ac * cof_ac
    places = lax.broadcasted_iota(jnp.int32, det.shape, 1)
    scale = jnp.where(places < counts, 1.0, 0.0) / det
    rows = ((cof_aa, cof_ab, cof_ac), (cof_ab, cof_bb, cof_bc), (cof_ac, cof_bc, cof_cc))
    return [[entry * scale for entry in row] for row in rows]


def slot_pair(first, second, coef, s, flips):
    params, points = first.shape[-1] // 2, first.shape[-2]
    turned = [
        jnp.transpose(jnp.concatenate([first[e][:, params:], second[e][:, params:]], axis=1)).astype(jnp.float32) for e in range(3)
    ]
    mirrored = []
    for i, jac in enumerate((first, second)):
        right = [comp[i * params : (i + 1) * params] for comp in turned]
        row = slice(s + i, s + i + 1)
        solved = [
            (coef[c][0][row] * right[0] + coef[c][1][row] * right[1] + coef[c][2][row] * right[2]).astype(jnp.bfloat16)
            for c in range(3)
        ]
        block = jnp.dot(
            jnp.concatenate(solved, axis=1), jac.reshape(3 * points, 2 * params), preferred_element_type=jnp.float32
        )
        mirrored.append(block[:, :params])
    straight = jnp.transpose(jnp.concatenate(mirrored, axis=1))
    return [
        jnp.where(flips[s + i : s + i + 1, :params] > 0, mirrored[i], straight[i * params : (i + 1) * params]) for i in range(2)
    ]


def each(low, high, body):
    def step(i, carry):
        body(i)
        return carry

    lax.fori_loop(low, high, step, 0)


def reduce_kernel(
    jac_hbm, normals_ref, counts_ref, flip_ref, ids_ref, couple_ref, fin_ref,
    jac_v, send, arrived, ids_all, hot, halves, dense, passing, stage, scratch,
    jac_sem, ids_ssem, ids_rsem, a_ssem, a_rsem, b_ssem, b_rsem, c_ssem, c_rsem, own_sem,
):
    groups, cell, tiles, orbits = jac_sem.shape[0], arrived.shape[0], dense.shape[0], couple_ref.shape[0]
    units, share, rank = fin_ref.shape[1], fin_ref.shape[2], dense.shape[2]
    slots, params = jac_v.shape[0], jac_v.shape[3] // 2
    step, half_rows = slots // groups, params // 2
    near = cell // orbits
    teams = tiles // near
    t, o = lax.axis_index("tile"), lax.axis_index("orbit")
    team, seat = t // near, lax.rem(t, near)
    me = seat * orbits + o

    def peer_of(k):
        return lax.rem(me + k, cell)

    def place(member):
        return (team * near + member // orbits, lax.rem(member, orbits))

    def team_of(k):
        return lax.rem(team + k, teams)

    def jac_copy(g):
        rows = pl.ds(pl.multiple_of(g * step, step), step)
        return pltpu.make_async_copy(jac_hbm.at[rows], jac_v.at[rows], jac_sem.at[g])

    def ids_copy(peer, src):
        return pltpu.make_async_remote_copy(
            src_ref=ids_ref, dst_ref=ids_all.at[src], send_sem=ids_ssem.at[peer], recv_sem=ids_rsem.at[src],
            device_id=place(peer), device_id_type=MESH)

    def block_copy(peer, src, g):
        rows = pl.ds(pl.multiple_of(g * step, step), step)
        return pltpu.make_async_remote_copy(
            src_ref=send.at[peer, rows], dst_ref=arrived.at[src, rows], send_sem=a_ssem.at[peer, g],
            recv_sem=a_rsem.at[src, g], device_id=place(peer), device_id_type=MESH)

    def sum_copy(to, src, i, u):
        return pltpu.make_async_remote_copy(
            src_ref=dense.at[to * near + i, u], dst_ref=passing.at[src, i, u], send_sem=b_ssem.at[to, i, u],
            recv_sem=b_rsem.at[src, i, u], device_id=(to * near + seat, o), device_id_type=MESH)

    def out_copy(peer, src, u):
        return pltpu.make_async_remote_copy(
            src_ref=stage.at[peer, u], dst_ref=fin_ref.at[src, u], send_sem=c_ssem.at[peer, u],
            recv_sem=c_rsem.at[src, u], device_id=place(peer), device_id_type=MESH)

    def own_copy(u):
        return pltpu.make_async_copy(stage.at[me, u], fin_ref.at[me, u], own_sem.at[u])

    each(0, groups, lambda g: jac_copy(g).start())
    barrier = pltpu.get_barrier_semaphore()
    each(1, cell, lambda k: pl.semaphore_signal(barrier, inc=1, device_id=place(peer_of(k)), device_id_type=MESH))
    each(1, teams, lambda k: pl.semaphore_signal(
        barrier, inc=1, device_id=(team_of(k) * near + seat, o), device_id_type=MESH))
    pl.semaphore_wait(barrier, cell - 1 + teams - 1)

    each(1, cell, lambda k: ids_copy(peer_of(k), me).start())
    ids_all[me] = ids_ref[...]

    def group(g):
        jac_copy(g).wait()
        at = pl.multiple_of(g * step, step)
        rows = pl.ds(at, step)
        coef = weights(normals_ref[:, rows, :], counts_ref[rows, :])
        flips = flip_ref[rows, :]
        for s in range(0, step, 2):
            for i, block in enumerate(slot_pair(jac_v[at + s], jac_v[at + s + 1], coef, s, flips)):
                scratch[(s + i) * params : (s + i + 1) * params, :] = block
        for unit in range(cell * units):
            pieces = [scratch[pl.ds(unit + half * half_rows, step, stride=params), :] for half in range(2)]
            c, u = divmod(unit, units)
            send[c, rows, u * LANES : (u + 1) * LANES] = jnp.concatenate(pieces, axis=1)
        arrived[me, rows, :] = send[me, rows, :]
        each(1, cell, lambda k: block_copy(peer_of(k), me, g).start())

    each(0, groups, group)

    each(1, cell, lambda k: ids_copy(peer_of(k), peer_of(k)).wait_recv())

    def fill_hot(d):
        want = lax.broadcasted_iota(jnp.int32, (rank, slots), 0) + d * rank
        for p in range(cell):
            hot[d, :, p * slots : (p + 1) * slots] = jnp.where(want == ids_all[p, 0:1, :], 1.0, 0.0).astype(jnp.bfloat16)

    each(0, tiles, fill_hot)
    each(1, cell, lambda k: each(0, groups, lambda g: block_copy(peer_of(k), peer_of(k), g).wait_recv()))

    def add_up(d, u):
        both = jnp.dot(hot[d], halves[u], preferred_element_type=jnp.float32)
        dense[d, u] = both[:, :LANES] + both[:, LANES:]

    for u in range(units):
        found = arrived[:, :, u * LANES : (u + 1) * LANES].reshape(cell * slots, LANES)
        high = found.astype(jnp.bfloat16)
        low = (found - high.astype(jnp.float32)).astype(jnp.bfloat16)
        halves[u, :, :LANES] = high
        halves[u, :, LANES:] = low

        def away(n):
            to, i = team_of(1 + n // near), lax.rem(n, near)
            add_up(to * near + i, u)
            sum_copy(to, team, i, u).start()

        each(0, (teams - 1) * near, away)

    each(0, units, lambda u: each(0, near, lambda i: add_up(team * near + i, u)))

    def finish(n):
        u, i = n // near, lax.rem(n, near)
        d = team * near + i

        def gather_in(k):
            src = team_of(k)
            sum_copy(src, src, i, u).wait_recv()
            dense[d, u] = dense[d, u] + passing[src, i, u]

        each(1, teams, gather_in)

        def hand_out(k):
            member = i * orbits + k
            wanted = couple_ref[k][0:1, :]
            taken = dense[d, u, 0:share, :]
            for c in range(1, orbits // 2):
                taken = jnp.where(wanted == c, dense[d, u, c * share : (c + 1) * share, :], taken)
            stage[member, u] = taken

            @pl.when(member != me)
            def _():
                out_copy(member, me, u).start()

            @pl.when(member == me)
            def _():
                own_copy(u).start()

        each(0, orbits, hand_out)

    each(0, units * near, finish)

    def settle(u):
        own_copy(u).wait()
        each(1, cell, lambda k: out_copy(peer_of(k), peer_of(k), u).wait_recv())
        each(1, cell, lambda k: out_copy(peer_of(k), me, u).wait_send())
        each(1, teams, lambda k: each(0, near, lambda i: sum_copy(team_of(k), team, i, u).wait_send()))

    each(0, units, settle)
    each(1, cell, lambda k: ids_copy(peer_of(k), me).wait_send())
    each(1, cell, lambda k: each(0, groups, lambda g: block_copy(peer_of(k), me, g).wait_send()))


def reduced_parts(jac, normals, counts, flip, ids, couple, orbits, tiles):
    slots, _, points, both = jac.shape
    params = both // 2
    step = min(16, slots)
    groups = slots // step
    near = 2 if tiles % 2 == 0 and params * params % (2 * orbits * LANES) == 0 else 1
    cell, teams = near * orbits, tiles // near
    units = params * params // LANES // cell
    share = PAIR_ORB // tiles
    rank = orbits // 2 * share
    vmem = pl.BlockSpec(memory_space=pltpu.VMEM)
    f32 = jnp.float32
    dma = pltpu.SemaphoreType.DMA
    return pl.pallas_call(
        reduce_kernel,
        in_specs=[pl.BlockSpec(memory_space=pl.ANY), vmem, vmem, vmem, vmem, vmem],
        out_specs=pl.BlockSpec(memory_space=pl.ANY),
        out_shape=jax.ShapeDtypeStruct((cell, units, share, LANES), f32),
        scratch_shapes=[
            pltpu.VMEM(jac.shape, jac.dtype),
            pltpu.VMEM((cell, slots, units * LANES), f32),
            pltpu.VMEM((cell, slots, units * LANES), f32),
            pltpu.VMEM((cell,) + ids.shape, jnp.int32),
            pltpu.VMEM((tiles, rank, cell * slots), jnp.bfloat16),
            pltpu.VMEM((units, cell * slots, 2 * LANES), jnp.bfloat16),
            pltpu.VMEM((tiles, units, rank, LANES), f32),
            pltpu.VMEM((teams, near, units, rank, LANES), f32),
            pltpu.VMEM((cell, units, share, LANES), f32),
            pltpu.VMEM((step * params, params), f32),
            dma((groups,)),
            dma((cell,)),
            dma((cell,)),
            dma((cell, groups)),
            dma((cell, groups)),
            dma((teams, near, units)),
            dma((teams, near, units)),
            dma((cell, units)),
            dma((cell, units)),
            dma((units,)),
        ],
        compiler_params=pltpu.CompilerParams(
            collective_id=0, has_side_effects=True, vmem_limit_bytes=48 * 1024 * 1024
        ),
    )(jac, normals, counts, flip, ids, couple)


def assemble_kernel(lead_ref, fin_ref, out_ref, turned):
    count, share, _ = fin_ref.shape
    params = 2 * count
    half = LANES // 2

    @pl.when(lead_ref[0] > 0)
    def _():
        for m in range(count):
            first = (2 * m) % count
            side = (2 * m) // count * half
            out_ref[:, m * LANES : (m + 1) * LANES] = jnp.concatenate(
                [fin_ref[first + i, :, side : side + half] for i in range(2)], axis=1
            )

    @pl.when(lead_ref[0] == 0)
    def _():
        for unit in range(count):
            turned[unit * LANES : (unit + 1) * LANES, :] = jnp.transpose(fin_ref[unit])
        for m in range(count):
            rows = [turned[pl.ds(2 * m + k + h * params, count, stride=LANES), :] for k in range(2) for h in range(2)]
            out_ref[:, m * LANES : (m + 1) * LANES] = jnp.transpose(jnp.concatenate(rows, axis=0))


def assembled(lead, fin):
    count, share, _ = fin.shape
    vmem = pl.BlockSpec(memory_space=pltpu.VMEM)
    return pl.pallas_call(
        assemble_kernel,
        in_specs=[pl.BlockSpec(memory_space=pltpu.SMEM), vmem],
        out_specs=vmem,
        out_shape=jax.ShapeDtypeStruct((share, count * LANES), jnp.float32),
        scratch_shapes=[pltpu.VMEM((count * LANES, share), jnp.float32)],
        compiler_params=pltpu.CompilerParams(vmem_limit_bytes=16 * 1024 * 1024),
    )(lead, fin)


def local(jacobians, point_normals, block_counts, pair_owner, pair_local, crossing):
    slots, points, _, both = jacobians.shape
    orbits, tiles = lax.axis_size("orbit"), lax.axis_size("tile")
    couples, share = orbits // 2, PAIR_ORB // tiles
    jac = jnp.transpose(jacobians, (0, 2, 1, 3))
    normals = jnp.transpose(point_normals, (1, 0, 2))
    counts = jnp.broadcast_to(block_counts[0][:, None], (slots, points))
    orbit_ids = jnp.arange(orbits, dtype=jnp.int32)
    leads = orbit_ids < crossing
    couple = jnp.sum((orbit_ids[None, :] < jnp.minimum(orbit_ids, crossing)[:, None]) & leads[None, :], axis=1).astype(jnp.int32)
    owner_hot = pair_owner == orbit_ids[None, :]
    slot_couple = jnp.sum(jnp.where(owner_hot, couple[None, :], 0), axis=1)
    flip = jnp.sum(jnp.where(owner_hot & ~leads[None, :], 1, 0), axis=1)
    flip = jnp.broadcast_to(flip[:, None], (slots, points))
    row = (pair_local // share) * (couples * share) + slot_couple * share + pair_local % share
    ids = jnp.broadcast_to(row[None, :], (8, slots))
    wanted = jnp.broadcast_to(couple[:, None, None], (orbits, 8, LANES))
    fin = reduced_parts(jac, normals, counts, flip, ids, wanted, orbits, tiles)
    lead = leads[lax.axis_index("orbit")].astype(jnp.int32).reshape(1)
    return assembled(lead, fin.reshape(-1, share, LANES))[None]


def solution(mesh):
    in_specs = (
        P(("tile", "orbit"), None, None, None),
        P(("tile", "orbit"), None, None),
        P(("tile", "orbit"), None),
        P(("tile", "orbit"), None),
        P(("tile", "orbit")),
        P(),
    )
    out_specs = P("orbit", "tile", None)
    return jax.shard_map(local, mesh=mesh, in_specs=in_specs, out_specs=out_specs, check_vma=False)
```

time: 95 us -> 79 us (0.83)
  the two profiles are of different devices: /device:TPU:5 before, /device:TPU:15 now
where the time goes in v3:
time: 79 us; the launch traced here: 78.8 us
  Pallas kernels  72.7 us (92%)
  other arithmetic  2.91 us (4%)
  local copies, waits for them, and re-layouts  2.48 us (3%)
    pallas_call x1, Pallas kernels, reduced_parts(): pl.pallas_call(reduce_kernel, in_specs=[pl.BlockSpec(memory_space=pl.ANY)...  69.9 us
    pallas_call x1, Pallas kernels, assembled(): pl.pallas_call(assemble_kernel, in_specs=[pl.BlockSpec(memory_space=pltpu...  2.78 us

profile of v3, /device:TPU:15, one launch (start us, length us, event | category | flops | bytes accessed | tf_op | source)
XLA Modules:
  0.0 78.8 jit_solution(11391907420964886465)
XLA Ops:
  0.0 0.7 iota_minimum_fusion
  0.7 0.7 fusion.3
  1.3 0.6 dynamic_slice.3
  2.6 0.2 convert_reduce_fusion
  2.7 0.7 select_reduce_fusion
  3.5 0.7 fusion.2
  4.2 0.1 broadcast_in_dim.59.couple_ref
  4.2 0.1 broadcast_in_dim.56.flip_ref
  4.3 0.7 broadcast_in_dim.31.counts_ref
  5.1 0.0 copy-start
  5.1 1.0 %copy-done = f32[128,6,128]{2,0,1:T(8,128)S(1)} copy-done((f32[128,6,128]{2,0,1:T(8,128)S(1)}, f32[128,6,128]{2,0,1:T(8,128)}, u32[]{:S(2)}) %copy-start) | copy-done | bytes 393240
  6.1 69.9 %shard_map.64 = f32[16,2,64,128]{3,2,1,0:T(8,128)S(1)} custom-call(bf16[128,3,128,128]{3,2,1,0:T(8,128)(2,1)} %bitcast.8, f32[6,128,128]{2,1,0:T(8,128)S(1)} %bitcast.7, s32[128,128]{1,0:T(8,128)S(1)} %broadcast_in_dim.31.counts_ref, s32[128,128]{1,0:T(8,128)S(1)} %broadcast_in_dim.56.flip_ref, s32[8,128]{1,0:T(8,128)S(1)} %broadcast_in_dim.58.ids_ref, ...), custom_call_target="tpu_custom_call" | custom-call | tf_op jit(solution)/shard_map/pallas_call | solution.py:224
  76.0 2.8 %shard_map.65 = f32[64,4096]{1,0:T(8,128)} custom-call(s32[1]{0:T(128)S(6)} %convert_element_type.7.lead_ref, f32[32,64,128]{2,1,0:T(8,128)S(1)} %bitcast.6), custom_call_target="tpu_custom_call" | custom-call | tf_op jit(solution)/shard_map/pallas_call | solution.py:283
  (1 shorter events, 0.0 us)
Async XLA Ops:
  5.1 1.0 %copy-start = (f32[128,6,128]{2,0,1:T(8,128)S(1)}, f32[128,6,128]{2,0,1:T(8,128)}, u32[]{:S(2)}) copy-start(f32[128,6,128]{2,0,1:T(8,128)} %param.7) | copy-start | bytes 1179652

commit v4 on v3

--- a/solution.py
+++ b/solution.py
@@ -19,7 +19,7 @@
     cof_ac = ab * bc - ac * d2
     cof_bc = ab * ac - d1 * bc
     det = d1 * cof_aa + ab * cof_ab + ac * cof_ac
-    places = lax.broadcasted_iota(jnp.int32, det.shape, 1)
+    places = lax.broadcasted_iota(jnp.int32, det.shape, 1).astype(jnp.float32)
     scale = jnp.where(places < counts, 1.0, 0.0) / det
     rows = ((cof_aa, cof_ab, cof_ac), (cof_ab, cof_bb, cof_bc), (cof_ac, cof_bc, cof_cc))
     return [[entry * scale for entry in row] for row in rows]
@@ -57,11 +57,11 @@
 
 
 def reduce_kernel(
-    jac_hbm, normals_ref, counts_ref, flip_ref, ids_ref, couple_ref, fin_ref,
-    jac_v, send, arrived, ids_all, hot, halves, dense, passing, stage, scratch,
-    jac_sem, ids_ssem, ids_rsem, a_ssem, a_rsem, b_ssem, b_rsem, c_ssem, c_rsem, own_sem,
+    jac_hbm, normals_hbm, counts_ref, owner_ref, local_ref, crossing_ref, fin_ref,
+    normals_v, counts_v, flip_v, ids_v, couple_v, jac_v, send, arrived, ids_all, hot, halves, dense, passing, stage, scratch,
+    normals_sem, jac_sem, ids_ssem, ids_rsem, a_ssem, a_rsem, b_ssem, b_rsem, c_ssem, c_rsem, own_sem,
 ):
-    groups, cell, tiles, orbits = jac_sem.shape[0], arrived.shape[0], dense.shape[0], couple_ref.shape[0]
+    groups, cell, tiles, orbits = jac_sem.shape[0], arrived.shape[0], dense.shape[0], crossing_ref.shape[0]
     units, share, rank = fin_ref.shape[1], fin_ref.shape[2], dense.shape[2]
     slots, params = jac_v.shape[0], jac_v.shape[3] // 2
     step, half_rows = slots // groups, params // 2
@@ -86,7 +86,7 @@
 
     def ids_copy(peer, src):
         return pltpu.make_async_remote_copy(
-            src_ref=ids_ref, dst_ref=ids_all.at[src], send_sem=ids_ssem.at[peer], recv_sem=ids_rsem.at[src],
+            src_ref=ids_v, dst_ref=ids_all.at[src], send_sem=ids_ssem.at[peer], recv_sem=ids_rsem.at[src],
             device_id=place(peer), device_id_type=MESH)
 
     def block_copy(peer, src, g):
@@ -108,22 +108,44 @@
     def own_copy(u):
         return pltpu.make_async_copy(stage.at[me, u], fin_ref.at[me, u], own_sem.at[u])
 
+    normals_copy = pltpu.make_async_copy(normals_hbm, normals_v, normals_sem)
+    normals_copy.start()
     each(0, groups, lambda g: jac_copy(g).start())
     barrier = pltpu.get_barrier_semaphore()
     each(1, cell, lambda k: pl.semaphore_signal(barrier, inc=1, device_id=place(peer_of(k)), device_id_type=MESH))
     each(1, teams, lambda k: pl.semaphore_signal(
         barrier, inc=1, device_id=(team_of(k) * near + seat, o), device_id_type=MESH))
+
+    points = normals_v.shape[2]
+    lead = [(k < crossing_ref[k]).astype(jnp.int32) for k in range(orbits)]
+    first = [jnp.minimum(k, crossing_ref[k]) for k in range(orbits)]
+    couple = [sum(lead[j] * (j < first[k]).astype(jnp.int32) for j in range(orbits)) for k in range(orbits)]
+    owner = jnp.broadcast_to(owner_ref[...], ids_v.shape)
+    where = jnp.broadcast_to(local_ref[...], ids_v.shape)
+    slot_couple, slot_flip, slot_tile = (jnp.zeros(ids_v.shape, jnp.int32) for _ in range(3))
+    for k in range(orbits):
+        hit = (owner == k).astype(jnp.int32)
+        slot_couple = slot_couple + hit * couple[k]
+        slot_flip = slot_flip + hit * (1 - lead[k])
+        couple_v[k] = jnp.full(couple_v.shape[1:], couple[k], jnp.int32)
+    for d in range(1, tiles):
+        slot_tile = slot_tile + (where >= d * share).astype(jnp.int32)
+    ids_v[...] = slot_tile * rank + slot_couple * share + where - slot_tile * share
+    for column, row in ((flip_v, slot_flip[0:1]), (counts_v, counts_ref[...])):
+        column[...] = jnp.transpose(jnp.broadcast_to(row.astype(jnp.float32), (points, slots)))
+
     pl.semaphore_wait(barrier, cell - 1 + teams - 1)
 
     each(1, cell, lambda k: ids_copy(peer_of(k), me).start())
-    ids_all[me] = ids_ref[...]
+    ids_all[me] = ids_v[...]
+    normals_copy.wait()
 
     def group(g):
         jac_copy(g).wait()
         at = pl.multiple_of(g * step, step)
         rows = pl.ds(at, step)
-        coef = weights(normals_ref[:, rows, :], counts_ref[rows, :])
-        flips = flip_ref[rows, :]
+        coef = weights(normals_v[:, rows, :], counts_v[rows, :])
+        flips = flip_v[rows, :]
         for s in range(0, step, 2):
             for i, block in enumerate(slot_pair(jac_v[at + s], jac_v[at + s + 1], coef, s, flips)):
                 scratch[(s + i) * params : (s + i + 1) * params, :] = block
@@ -138,17 +160,24 @@
 
     each(1, cell, lambda k: ids_copy(peer_of(k), peer_of(k)).wait_recv())
 
-    def fill_hot(d):
-        want = lax.broadcasted_iota(jnp.int32, (rank, slots), 0) + d * rank
+    def fill_hot(who, i):
+        rows = slice(i * rank, (i + 1) * rank)
+        want = lax.broadcasted_iota(jnp.int32, (rank, slots), 0) + (who * near + i) * rank
         for p in range(cell):
-            hot[d, :, p * slots : (p + 1) * slots] = jnp.where(want == ids_all[p, 0:1, :], 1.0, 0.0).astype(jnp.bfloat16)
-
-    each(0, tiles, fill_hot)
+            hot[who, rows, p * slots : (p + 1) * slots] = jnp.where(want == ids_all[p, 0:1, :], 1.0, 0.0).astype(jnp.bfloat16)
+
+    def fill_team(k):
+        for i in range(near):
+            fill_hot(team_of(k), i)
+
+    each(1, teams, fill_team)
     each(1, cell, lambda k: each(0, groups, lambda g: block_copy(peer_of(k), peer_of(k), g).wait_recv()))
 
-    def add_up(d, u):
-        both = jnp.dot(hot[d], halves[u], preferred_element_type=jnp.float32)
-        dense[d, u] = both[:, :LANES] + both[:, LANES:]
+    def add_up(who, u):
+        both = jnp.dot(hot[who], halves[u], preferred_element_type=jnp.float32)
+        both = both[:, :LANES] + both[:, LANES:]
+        for i in range(near):
+            dense[who * near + i, u] = both[i * rank : (i + 1) * rank]
 
     for u in range(units):
         found = arrived[:, :, u * LANES : (u + 1) * LANES].reshape(cell * slots, LANES)
@@ -157,14 +186,14 @@
         halves[u, :, :LANES] = high
         halves[u, :, LANES:] = low
 
-        def away(n):
-            to, i = team_of(1 + n // near), lax.rem(n, near)
-            add_up(to * near + i, u)
-            sum_copy(to, team, i, u).start()
-
-        each(0, (teams - 1) * near, away)
-
-    each(0, units, lambda u: each(0, near, lambda i: add_up(team * near + i, u)))
+        def away(k):
+            add_up(team_of(k), u)
+            each(0, near, lambda i: sum_copy(team_of(k), team, i, u).start())
+
+        each(1, teams, away)
+
+    fill_team(0)
+    each(0, units, lambda u: add_up(team, u))
 
     def finish(n):
         u, i = n // near, lax.rem(n, near)
@@ -179,7 +208,7 @@
 
         def hand_out(k):
             member = i * orbits + k
-            wanted = couple_ref[k][0:1, :]
+            wanted = couple_v[k][0:1, :]
             taken = dense[d, u, 0:share, :]
             for c in range(1, orbits // 2):
                 taken = jnp.where(wanted == c, dense[d, u, c * share : (c + 1) * share, :], taken)
@@ -208,8 +237,9 @@
     each(1, cell, lambda k: each(0, groups, lambda g: block_copy(peer_of(k), me, g).wait_send()))
 
 
-def reduced_parts(jac, normals, counts, flip, ids, couple, orbits, tiles):
+def reduced_parts(jac, normals, counts, owner, where, crossing, tiles):
     slots, _, points, both = jac.shape
+    orbits = crossing.shape[0]
     params = both // 2
     step = min(16, slots)
     groups = slots // step
@@ -223,20 +253,26 @@
     dma = pltpu.SemaphoreType.DMA
     return pl.pallas_call(
         reduce_kernel,
-        in_specs=[pl.BlockSpec(memory_space=pl.ANY), vmem, vmem, vmem, vmem, vmem],
+        in_specs=[pl.BlockSpec(memory_space=pl.ANY)] * 2 + [vmem] * 3 + [pl.BlockSpec(memory_space=pltpu.SMEM)],
         out_specs=pl.BlockSpec(memory_space=pl.ANY),
         out_shape=jax.ShapeDtypeStruct((cell, units, share, LANES), f32),
         scratch_shapes=[
+            pltpu.VMEM(normals.shape, f32),
+            pltpu.VMEM((slots, points), f32),
+            pltpu.VMEM((slots, points), f32),
+            pltpu.VMEM((8, slots), jnp.int32),
+            pltpu.VMEM((orbits, 8, LANES), jnp.int32),
             pltpu.VMEM(jac.shape, jac.dtype),
             pltpu.VMEM((cell, slots, units * LANES), f32),
             pltpu.VMEM((cell, slots, units * LANES), f32),
-            pltpu.VMEM((cell,) + ids.shape, jnp.int32),
-            pltpu.VMEM((tiles, rank, cell * slots), jnp.bfloat16),
+            pltpu.VMEM((cell, 8, slots), jnp.int32),
+            pltpu.VMEM((teams, near * rank, cell * slots), jnp.bfloat16),
             pltpu.VMEM((units, cell * slots, 2 * LANES), jnp.bfloat16),
             pltpu.VMEM((tiles, units, rank, LANES), f32),
             pltpu.VMEM((teams, near, units, rank, LANES), f32),
             pltpu.VMEM((cell, units, share, LANES), f32),
             pltpu.VMEM((step * params, params), f32),
+            pltpu.SemaphoreType.DMA,
             dma((groups,)),
             dma((cell,)),
             dma((cell,)),
@@ -251,15 +287,17 @@
         compiler_params=pltpu.CompilerParams(
             collective_id=0, has_side_effects=True, vmem_limit_bytes=48 * 1024 * 1024
         ),
-    )(jac, normals, counts, flip, ids, couple)
-
-
-def assemble_kernel(lead_ref, fin_ref, out_ref, turned):
+    )(jac, normals, counts, owner, where, crossing)
+
+
+def assemble_kernel(crossing_ref, fin_ref, out_ref, turned):
+    orbit = lax.axis_index("orbit")
+    leads = crossing_ref[orbit] > orbit
     count, share, _ = fin_ref.shape
     params = 2 * count
     half = LANES // 2
 
-    @pl.when(lead_ref[0] > 0)
+    @pl.when(leads)
     def _():
         for m in range(count):
             first = (2 * m) % count
@@ -268,7 +306,7 @@
                 [fin_ref[first + i, :, side : side + half] for i in range(2)], axis=1
             )
 
-    @pl.when(lead_ref[0] == 0)
+    @pl.when(jnp.logical_not(leads))
     def _():
         for unit in range(count):
             turned[unit * LANES : (unit + 1) * LANES, :] = jnp.transpose(fin_ref[unit])
@@ -277,7 +315,7 @@
             out_ref[:, m * LANES : (m + 1) * LANES] = jnp.transpose(jnp.concatenate(rows, axis=0))
 
 
-def assembled(lead, fin):
+def assembled(crossing, fin):
     count, share, _ = fin.shape
     vmem = pl.BlockSpec(memory_space=pltpu.VMEM)
     return pl.pallas_call(
@@ -287,29 +325,16 @@
         out_shape=jax.ShapeDtypeStruct((share, count * LANES), jnp.float32),
         scratch_shapes=[pltpu.VMEM((count * LANES, share), jnp.float32)],
         compiler_params=pltpu.CompilerParams(vmem_limit_bytes=16 * 1024 * 1024),
-    )(lead, fin)
+    )(crossing, fin)
 
 
 def local(jacobians, point_normals, block_counts, pair_owner, pair_local, crossing):
-    slots, points, _, both = jacobians.shape
-    orbits, tiles = lax.axis_size("orbit"), lax.axis_size("tile")
-    couples, share = orbits // 2, PAIR_ORB // tiles
+    tiles = lax.axis_size("tile")
     jac = jnp.transpose(jacobians, (0, 2, 1, 3))
     normals = jnp.transpose(point_normals, (1, 0, 2))
-    counts = jnp.broadcast_to(block_counts[0][:, None], (slots, points))
-    orbit_ids = jnp.arange(orbits, dtype=jnp.int32)
-    leads = orbit_ids < crossing
-    couple = jnp.sum((orbit_ids[None, :] < jnp.minimum(orbit_ids, crossing)[:, None]) & leads[None, :], axis=1).astype(jnp.int32)
-    owner_hot = pair_owner == orbit_ids[None, :]
-    slot_couple = jnp.sum(jnp.where(owner_hot, couple[None, :], 0), axis=1)
-    flip = jnp.sum(jnp.where(owner_hot & ~leads[None, :], 1, 0), axis=1)
-    flip = jnp.broadcast_to(flip[:, None], (slots, points))
-    row = (pair_local // share) * (couples * share) + slot_couple * share + pair_local % share
-    ids = jnp.broadcast_to(row[None, :], (8, slots))
-    wanted = jnp.broadcast_to(couple[:, None, None], (orbits, 8, LANES))
-    fin = reduced_parts(jac, normals, counts, flip, ids, wanted, orbits, tiles)
-    lead = leads[lax.axis_index("orbit")].astype(jnp.int32).reshape(1)
-    return assembled(lead, fin.reshape(-1, share, LANES))[None]
+    owner, where = pair_owner.reshape(1, -1), pair_local.reshape(1, -1)
+    fin = reduced_parts(jac, normals, block_counts, owner, where, crossing, tiles)
+    return assembled(crossing, fin.reshape(-1, PAIR_ORB // tiles, LANES))[None]
 
 
 def solution(mesh):

time: 79 us -> 79.7 us (level)
  Pallas kernels: 72.7 us -> 75.8 us
  other arithmetic: 2.91 us -> 0 us
  local copies, waits for them, and re-layouts: 2.48 us -> 3.61 us
    unnamed x2 -> x10, local copies, waits for them, and re-layouts: 1 us -> 3.61 us
    pallas_call x1, Pallas kernels: 69.9 us -> 72.5 us  [reduced_parts(): pl.pallas_call(reduce_kernel, in_specs=[pl.BlockSpec(memory_space=pl.ANY)...]
    reduce_sum x2 -> x0, other arithmetic: 0.93 us -> none  [the longest x1 0.74 us: local(): slot_couple = jnp.sum(jnp.where(owner_hot, couple[None, :], 0), axis=1)]
    broadcast_in_dim x4 -> x0, local copies, waits for them, and re-layouts: 0.89 us -> none  [the longest x1 0.74 us: local(): counts = jnp.broadcast_to(block_counts[0][:, None], (slots, points))]
where the time goes in v4:
time: 79.7 us; the launch traced here: 79.5 us
  Pallas kernels  75.8 us (95%)
  local copies, waits for them, and re-layouts  3.61 us (5%)
    pallas_call x1, Pallas kernels, reduced_parts(): pl.pallas_call(reduce_kernel, in_specs=[pl.BlockSpec(memory_space=pl.ANY)...  72.5 us
    unnamed x10, local copies, waits for them, and re-layouts  3.61 us
    pallas_call x1, Pallas kernels, assembled(): pl.pallas_call(assemble_kernel, in_specs=[pl.BlockSpec(memory_space=pltpu...  3.32 us

profile of v4, /device:TPU:15, one launch (start us, length us, event | category | flops | bytes accessed | tf_op | source)
XLA Modules:
  0.0 79.5 jit_solution(13622419779156600532)
XLA Ops:
  0.0 0.0 copy-start
  0.0 1.0 %copy-done = f32[128,6,128]{2,0,1:T(8,128)S(1)} copy-done((f32[128,6,128]{2,0,1:T(8,128)S(1)}, f32[128,6,128]{2,0,1:T(8,128)}, u32[]{:S(2)}) %copy-start) | copy-done | bytes 393240
  1.0 0.0 copy-start.1
  1.0 0.7 copy-done.1
  1.7 0.0 copy-start.2
  1.7 0.7 copy-done.2
  2.3 0.0 copy-start.3
  2.3 0.7 copy-done.3
  3.0 0.0 copy-start.4
  3.0 0.7 copy-done.4
  3.6 72.5 %shard_map.64 = f32[16,2,64,128]{3,2,1,0:T(8,128)S(1)} custom-call(bf16[128,3,128,128]{3,2,1,0:T(8,128)(2,1)} %bitcast.10, f32[6,128,128]{2,1,0:T(8,128)S(1)} %bitcast.7, s32[1,128]{1,0:T(1,128)S(1)} %copy-done.2, s32[1,128]{1,0:T(1,128)S(1)} %bitcast.8, s32[1,128]{1,0:T(1,128)S(1)} %bitcast.9, s32[8]{0:T(128)S(1)} %copy-done.1), custom_call_target="tpu_custom_call" | custom-call | tf_op jit(solution)/shard_map/pallas_call | solution.py:254
  76.2 3.3 %shard_map.65 = f32[64,4096]{1,0:T(8,128)} custom-call(s32[8]{0:T(128)S(1)} %copy-done.1, f32[32,64,128]{2,1,0:T(8,128)S(1)} %bitcast.6), custom_call_target="tpu_custom_call" | custom-call | tf_op jit(solution)/shard_map/pallas_call | solution.py:321
Async XLA Ops:
  0.0 1.0 %copy-start = (f32[128,6,128]{2,0,1:T(8,128)S(1)}, f32[128,6,128]{2,0,1:T(8,128)}, u32[]{:S(2)}) copy-start(f32[128,6,128]{2,0,1:T(8,128)} %param.7) | copy-start | bytes 1179652
  1.0 0.7 copy-start.1
  1.7 0.7 copy-start.2
  2.3 0.7 copy-start.3
  3.0 0.7 copy-start.4

commit v5 on v4

--- a/solution.py
+++ b/solution.py
@@ -57,14 +57,16 @@
 
 
 def reduce_kernel(
-    jac_hbm, normals_hbm, counts_ref, owner_ref, local_ref, crossing_ref, fin_ref,
-    normals_v, counts_v, flip_v, ids_v, couple_v, jac_v, send, arrived, ids_all, hot, halves, dense, passing, stage, scratch,
-    normals_sem, jac_sem, ids_ssem, ids_rsem, a_ssem, a_rsem, b_ssem, b_rsem, c_ssem, c_rsem, own_sem,
+    jac_hbm, normals_hbm, counts_hbm, owner_hbm, local_hbm, crossing_ref, fin_ref,
+    counts_ref, owner_ref, local_ref, normals_v, counts_v, flip_v, ids_v, couple_v, jac_v, send, arrived, ids_all, hot, halves, dense, passing, stage, scratch,
+    small_sem, normals_sem, jac_sem, ids_ssem, ids_rsem, a_ssem, a_rsem, b_ssem, b_rsem, c_ssem, c_rsem, own_sem,
 ):
-    groups, cell, tiles, orbits = jac_sem.shape[0], arrived.shape[0], dense.shape[0], crossing_ref.shape[0]
+    groups, cell, tiles, orbits = jac_sem.shape[0], arrived.shape[1], dense.shape[0], crossing_ref.shape[0]
     units, share, rank = fin_ref.shape[1], fin_ref.shape[2], dense.shape[2]
     slots, params = jac_v.shape[0], jac_v.shape[3] // 2
     step, half_rows = slots // groups, params // 2
+    batches = max(1, groups // 2)
+    batch = slots // batches
     near = cell // orbits
     teams = tiles // near
     t, o = lax.axis_index("tile"), lax.axis_index("orbit")
@@ -89,11 +91,16 @@
             src_ref=ids_v, dst_ref=ids_all.at[src], send_sem=ids_ssem.at[peer], recv_sem=ids_rsem.at[src],
             device_id=place(peer), device_id_type=MESH)
 
-    def block_copy(peer, src, g):
-        rows = pl.ds(pl.multiple_of(g * step, step), step)
+    def block_copy(peer, src, u, rows):
         return pltpu.make_async_remote_copy(
-            src_ref=send.at[peer, rows], dst_ref=arrived.at[src, rows], send_sem=a_ssem.at[peer, g],
-            recv_sem=a_rsem.at[src, g], device_id=place(peer), device_id_type=MESH)
+            src_ref=send.at[u, peer, rows], dst_ref=arrived.at[u, src, rows], send_sem=a_ssem.at[u, peer],
+            recv_sem=a_rsem.at[u, src], device_id=place(peer), device_id_type=MESH)
+
+    whole_slots = pl.ds(0, slots)
+
+    def send_batch(u, n):
+        rows = pl.ds(pl.multiple_of(n * batch, batch), batch)
+        each(1, cell, lambda k: block_copy(peer_of(k), me, u, rows).start())
 
     def sum_copy(to, src, i, u):
         return pltpu.make_async_remote_copy(
@@ -109,6 +116,12 @@
         return pltpu.make_async_copy(stage.at[me, u], fin_ref.at[me, u], own_sem.at[u])
 
     normals_copy = pltpu.make_async_copy(normals_hbm, normals_v, normals_sem)
+    small = [
+        pltpu.make_async_copy(src, dst, small_sem.at[i])
+        for i, (src, dst) in enumerate(((counts_hbm, counts_ref), (owner_hbm, owner_ref), (local_hbm, local_ref)))
+    ]
+    for copy in small:
+        copy.start()
     normals_copy.start()
     each(0, groups, lambda g: jac_copy(g).start())
     barrier = pltpu.get_barrier_semaphore()
@@ -120,6 +133,8 @@
     lead = [(k < crossing_ref[k]).astype(jnp.int32) for k in range(orbits)]
     first = [jnp.minimum(k, crossing_ref[k]) for k in range(orbits)]
     couple = [sum(lead[j] * (j < first[k]).astype(jnp.int32) for j in range(orbits)) for k in range(orbits)]
+    for copy in small:
+        copy.wait()
     owner = jnp.broadcast_to(owner_ref[...], ids_v.shape)
     where = jnp.broadcast_to(local_ref[...], ids_v.shape)
     slot_couple, slot_flip, slot_tile = (jnp.zeros(ids_v.shape, jnp.int32) for _ in range(3))
@@ -152,48 +167,59 @@
         for unit in range(cell * units):
             pieces = [scratch[pl.ds(unit + half * half_rows, step, stride=params), :] for half in range(2)]
             c, u = divmod(unit, units)
-            send[c, rows, u * LANES : (u + 1) * LANES] = jnp.concatenate(pieces, axis=1)
-        arrived[me, rows, :] = send[me, rows, :]
-        each(1, cell, lambda k: block_copy(peer_of(k), me, g).start())
-
-    each(0, groups, group)
+            send[u, c, rows, :] = jnp.concatenate(pieces, axis=1)
+        for u in range(units):
+            arrived[u, me, rows, :] = send[u, me, rows, :]
+
+    early = batches // 2
+
+    def run_batch(n):
+        each(n * (groups // batches), (n + 1) * (groups // batches), group)
+        send_batch(0, n)
+
+        @pl.when(n < early)
+        def _():
+            for u in range(1, units):
+                send_batch(u, n)
+
+    each(0, batches, run_batch)
+    for u in range(1, units):
+        each(early, batches, lambda n: send_batch(u, n))
 
     each(1, cell, lambda k: ids_copy(peer_of(k), peer_of(k)).wait_recv())
 
     def fill_hot(who, i):
-        rows = slice(i * rank, (i + 1) * rank)
         want = lax.broadcasted_iota(jnp.int32, (rank, slots), 0) + (who * near + i) * rank
         for p in range(cell):
-            hot[who, rows, p * slots : (p + 1) * slots] = jnp.where(want == ids_all[p, 0:1, :], 1.0, 0.0).astype(jnp.bfloat16)
+            hot[who, i, :, p * slots : (p + 1) * slots] = jnp.where(want == ids_all[p, 0:1, :], 1.0, 0.0).astype(jnp.bfloat16)
 
     def fill_team(k):
         for i in range(near):
             fill_hot(team_of(k), i)
 
     each(1, teams, fill_team)
-    each(1, cell, lambda k: each(0, groups, lambda g: block_copy(peer_of(k), peer_of(k), g).wait_recv()))
-
-    def add_up(who, u):
-        both = jnp.dot(hot[who], halves[u], preferred_element_type=jnp.float32)
-        both = both[:, :LANES] + both[:, LANES:]
-        for i in range(near):
-            dense[who * near + i, u] = both[i * rank : (i + 1) * rank]
+
+    def add_up(who, i, u):
+        both = jnp.dot(hot[who, i], halves[u], preferred_element_type=jnp.float32)
+        dense[who * near + i, u] = both[:, :LANES] + both[:, LANES:]
 
     for u in range(units):
-        found = arrived[:, :, u * LANES : (u + 1) * LANES].reshape(cell * slots, LANES)
+        each(1, cell, lambda k: block_copy(peer_of(k), peer_of(k), u, whole_slots).wait_recv())
+        found = arrived[u].reshape(cell * slots, LANES)
         high = found.astype(jnp.bfloat16)
         low = (found - high.astype(jnp.float32)).astype(jnp.bfloat16)
         halves[u, :, :LANES] = high
         halves[u, :, LANES:] = low
 
-        def away(k):
-            add_up(team_of(k), u)
-            each(0, near, lambda i: sum_copy(team_of(k), team, i, u).start())
-
-        each(1, teams, away)
+        def away(n):
+            to, i = team_of(1 + n // near), lax.rem(n, near)
+            add_up(to, i, u)
+            sum_copy(to, team, i, u).start()
+
+        each(0, (teams - 1) * near, away)
 
     fill_team(0)
-    each(0, units, lambda u: add_up(team, u))
+    each(0, units, lambda u: each(0, near, lambda i: add_up(team, i, u)))
 
     def finish(n):
         u, i = n // near, lax.rem(n, near)
@@ -234,7 +260,7 @@
 
     each(0, units, settle)
     each(1, cell, lambda k: ids_copy(peer_of(k), me).wait_send())
-    each(1, cell, lambda k: each(0, groups, lambda g: block_copy(peer_of(k), me, g).wait_send()))
+    each(1, cell, lambda k: each(0, units, lambda u: block_copy(peer_of(k), me, u, whole_slots).wait_send()))
 
 
 def reduced_parts(jac, normals, counts, owner, where, crossing, tiles):
@@ -248,36 +274,39 @@
     units = params * params // LANES // cell
     share = PAIR_ORB // tiles
     rank = orbits // 2 * share
-    vmem = pl.BlockSpec(memory_space=pltpu.VMEM)
     f32 = jnp.float32
     dma = pltpu.SemaphoreType.DMA
     return pl.pallas_call(
         reduce_kernel,
-        in_specs=[pl.BlockSpec(memory_space=pl.ANY)] * 2 + [vmem] * 3 + [pl.BlockSpec(memory_space=pltpu.SMEM)],
+        in_specs=[pl.BlockSpec(memory_space=pl.ANY)] * 5 + [pl.BlockSpec(memory_space=pltpu.SMEM)],
         out_specs=pl.BlockSpec(memory_space=pl.ANY),
         out_shape=jax.ShapeDtypeStruct((cell, units, share, LANES), f32),
         scratch_shapes=[
+            pltpu.VMEM(counts.shape, jnp.int32),
+            pltpu.VMEM(owner.shape, jnp.int32),
+            pltpu.VMEM(where.shape, jnp.int32),
             pltpu.VMEM(normals.shape, f32),
             pltpu.VMEM((slots, points), f32),
             pltpu.VMEM((slots, points), f32),
             pltpu.VMEM((8, slots), jnp.int32),
             pltpu.VMEM((orbits, 8, LANES), jnp.int32),
             pltpu.VMEM(jac.shape, jac.dtype),
-            pltpu.VMEM((cell, slots, units * LANES), f32),
-            pltpu.VMEM((cell, slots, units * LANES), f32),
+            pltpu.VMEM((units, cell, slots, LANES), f32),
+            pltpu.VMEM((units, cell, slots, LANES), f32),
             pltpu.VMEM((cell, 8, slots), jnp.int32),
-            pltpu.VMEM((teams, near * rank, cell * slots), jnp.bfloat16),
+            pltpu.VMEM((teams, near, rank, cell * slots), jnp.bfloat16),
             pltpu.VMEM((units, cell * slots, 2 * LANES), jnp.bfloat16),
             pltpu.VMEM((tiles, units, rank, LANES), f32),
             pltpu.VMEM((teams, near, units, rank, LANES), f32),
             pltpu.VMEM((cell, units, share, LANES), f32),
             pltpu.VMEM((step * params, params), f32),
+            dma((3,)),
             pltpu.SemaphoreType.DMA,
             dma((groups,)),
             dma((cell,)),
             dma((cell,)),
-            dma((cell, groups)),
-            dma((cell, groups)),
+            dma((units, cell)),
+            dma((units, cell)),
             dma((teams, near, units)),
             dma((teams, near, units)),
             dma((cell, units)),
@@ -285,7 +314,7 @@
             dma((units,)),
         ],
         compiler_params=pltpu.CompilerParams(
-            collective_id=0, has_side_effects=True, vmem_limit_bytes=48 * 1024 * 1024
+            collective_id=0, has_side_effects=True, vmem_limit_bytes=60 * 1024 * 1024
         ),
     )(jac, normals, counts, owner, where, crossing)
 

time: 79.7 us -> 74.4 us (0.934)
  Pallas kernels: 75.8 us -> 73 us
  local copies, waits for them, and re-layouts: 3.61 us -> 1.22 us
    pallas_call x1, Pallas kernels: 72.5 us -> 69.6 us  [reduced_parts(): pl.pallas_call(reduce_kernel, in_specs=[pl.BlockSpec(memory_space=pl.ANY)...]
    unnamed x10 -> x4, local copies, waits for them, and re-layouts: 3.61 us -> 1.22 us
where the time goes in v5:
time: 74.4 us; the launch traced here: 74.2 us
  Pallas kernels  73 us (98%)
  local copies, waits for them, and re-layouts  1.22 us (2%)
    pallas_call x1, Pallas kernels, reduced_parts(): pl.pallas_call(reduce_kernel, in_specs=[pl.BlockSpec(memory_space=pl.ANY)...  69.6 us
    pallas_call x1, Pallas kernels, assembled(): pl.pallas_call(assemble_kernel, in_specs=[pl.BlockSpec(memory_space=pltpu...  3.31 us

profile of v5, /device:TPU:15, one launch (start us, length us, event | category | flops | bytes accessed | tf_op | source)
XLA Modules:
  0.0 74.2 jit_solution(6340255056118309083)
XLA Ops:
  0.0 0.0 copy-start.1
  0.0 69.6 %shard_map.64 = f32[16,2,64,128]{3,2,1,0:T(8,128)} custom-call(bf16[128,3,128,128]{3,2,1,0:T(8,128)(2,1)} %bitcast.7, f32[6,128,128]{2,1,0:T(8,128)} %bitcast.8, s32[1,128]{1,0:T(1,128)} %counts_hbm.1, s32[1,128]{1,0:T(1,128)} %bitcast.9, s32[1,128]{1,0:T(1,128)} %bitcast.10, s32[8]{0:T(128)} %crossing_ref.3), custom_call_target="tpu_custom_call" | custom-call | tf_op jit(solution)/shard_map/pallas_call | solution.py:279
  69.7 0.0 copy-done.1
  69.7 0.0 copy-start
  69.7 1.2 %copy-done = f32[16,2,64,128]{3,2,1,0:T(8,128)S(1)} copy-done((f32[16,2,64,128]{3,2,1,0:T(8,128)S(1)}, f32[16,2,64,128]{3,2,1,0:T(8,128)}, u32[]{:S(2)}) %copy-start) | copy-done | bytes 1048600
  70.9 3.3 %shard_map.65 = f32[64,4096]{1,0:T(8,128)} custom-call(s32[8]{0:T(128)S(1)} %copy-done.1, f32[32,64,128]{2,1,0:T(8,128)S(1)} %bitcast.6), custom_call_target="tpu_custom_call" | custom-call | tf_op jit(solution)/shard_map/pallas_call | solution.py:350
Async XLA Ops:
  0.0 69.7 %copy-start.1 = (s32[8]{0:T(128)S(1)}, s32[8]{0:T(128)}, u32[]{:S(2)}) copy-start(s32[8]{0:T(128)} %crossing_ref.3) | copy-start | bytes 100
  69.7 1.2 %copy-start = (f32[16,2,64,128]{3,2,1,0:T(8,128)S(1)}, f32[16,2,64,128]{3,2,1,0:T(8,128)}, u32[]{:S(2)}) copy-start(f32[16,2,64,128]{3,2,1,0:T(8,128)} %shard_map.64) | copy-start | bytes 3145732
